TPU v7x, 32 devices: a whole 2x2x4 slice. The times are simulated.
32 devices in a mesh: gx: 8 (over y, x, core), gy: 4 (over z).
Axes of the slice: x: 2, y: 2, z: 4, core: 2. Of those that a mesh axis runs over, the one named last changes fastest.
Arguments:
- tokens: bfloat16 [16384, 1024], P(('gx', 'gy')), may hold values from -6 to 6
- expert_ids: int32 [16384, 2], P(('gx', 'gy')), may hold values from 0 to 15, as said below
- gain_attn: bfloat16 [1024], P('gx'), may hold values from 0.099609375 to 1.8984375
- w_qkv: bfloat16 [3, 1024, 1024], P(None, 'gx', 'gy'), may hold values from -0.1875 to 0.1875
- w_out: bfloat16 [1024, 1024], P('gy', 'gx'), may hold values from -1.796875 to 1.796875
- rel_bias: bfloat16 [32, 16], P('gx', 'gy'), may hold values from -4 to 4
- gain_ffn: bfloat16 [1024], P('gx'), may hold values from 0.099609375 to 1.8984375
- router: bfloat16 [1024, 16], P('gx'), may hold values from -0.125 to 0.125
- w_in: bfloat16 [16, 1024, 5632], P('gy', 'gx'), may hold values from -0.1875 to 0.1875
- w_down: bfloat16 [16, 2816, 1024], P('gy', None, 'gx'), may hold values from -0.8984375 to 0.8984375
- cotangent: bfloat16 [16384, 1024], P(('gx', 'gy')), may hold values from -6 to 6
Outputs:
- mixed: bfloat16 [16384, 1024], P(('gx', 'gy'))
- loss: float32 [], replicated
- router_load: float32 [2, 16], replicated
- grad_tokens: float32 [16384, 1024], P(('gx', 'gy'))
- grad_gain_attn: float32 [1024], P('gx')
- grad_w_qkv: float32 [3, 1024, 1024], P(None, 'gx', 'gy')
- grad_w_out: float32 [1024, 1024], P('gy', 'gx')
- grad_rel_bias: float32 [32, 16], P('gx', 'gy')
- grad_gain_ffn: float32 [1024], P('gx')
- grad_router: float32 [1024, 16], P('gx')
- grad_w_in: float32 [16, 1024, 5632], P('gy', 'gx')
- grad_w_down: float32 [16, 2816, 1024], P('gy', None, 'gx')
Inputs may be any that keep to these rules, and one draw needn't show every extreme that they name: `expert_ids`: each row names 2 different experts; every expert is named by some row.
All inputs are finite; a program needn't handle non-finite values.
Results may differ from a plain program's by a relative error of at most 0.029.
Values may be sent and summed in bfloat16 or wider, within the bound.
A program may use at most 320 MiB of HBM per device.

v0:
```python
import functools
import math

import jax
import jax.numpy as jnp
from jax import lax
from jax.experimental import pallas as pl
from jax.experimental.pallas import tpu as pltpu
from jax.sharding import PartitionSpec as P

LEN = 1024
BLK = 256
CAP = 80


bucket_edges = (12, 16, 23, 32, 46, 64, 91)
epsilon = 1e-06
loss_weight = 0.01
masked_score = -1e30


def bucket_of(offset):
    magnitude = jnp.abs(offset)
    far_bucket = 8 + sum(
        ((magnitude >= edge_value).astype(jnp.int32) for edge_value in bucket_edges)
    )
    return jnp.where(magnitude < 8, magnitude, far_bucket) + 16 * (offset > 0).astype(jnp.int32)


def normalize(values):
    row_scale = lax.rsqrt(jnp.mean(values * values, axis=-1, keepdims=True) + epsilon)
    return (values * row_scale, row_scale)


def norm_back(grad_out, normed, row_scale, gain_vector):
    grad_normed = grad_out * gain_vector
    grad_gain = jnp.sum(grad_out * normed, axis=0)
    grad_input = row_scale * (
        grad_normed - normed * jnp.mean(grad_normed * normed, axis=-1, keepdims=True)
    )
    return (grad_input, grad_gain)


def spread_offsets(along_offsets, row_count):
    head_count, span_width = along_offsets.shape
    key_count = span_width - row_count + 1
    tiled_rows = jnp.broadcast_to(
        along_offsets[:, None, :], (head_count, row_count, span_width)
    ).reshape(head_count, row_count * span_width)
    padded = jnp.pad(tiled_rows, ((0, 0), (0, row_count)))
    shaped = padded.reshape(head_count, row_count, span_width + 1)[:, :, :key_count]
    return shaped[:, :, ::-1]


def gather_offsets(score_grid, row_count):
    head_count = score_grid.shape[0]
    key_count = score_grid.shape[2]
    span_width = key_count + row_count - 1
    padded = jnp.pad(score_grid[:, :, ::-1], ((0, 0), (0, 0), (0, row_count)))
    flat_rows = padded.reshape(head_count, row_count * (key_count + row_count))[
        :, : row_count * span_width
    ]
    return jnp.sum(flat_rows.reshape(head_count, row_count, span_width), axis=1)


def offset_table(q_start, row_count, key_count, bucket_count):
    spot_index = jnp.arange(key_count + row_count - 1, dtype=jnp.int32)
    offsets = key_count - 1 - spot_index - q_start
    return (
        bucket_of(offsets)[:, None] == jnp.arange(bucket_count, dtype=jnp.int32)[None, :]
    ).astype(jnp.float32)


def block_scores(query_rows, key_rows, table_float, q_start):
    row_count = query_rows.shape[0]
    depth = query_rows.shape[2]
    key_count = key_rows.shape[0]
    picks_table = offset_table(q_start, row_count, key_count, table_float.shape[0])
    along_offsets = jnp.dot(picks_table, table_float, precision=lax.Precision.HIGHEST).T
    bias_grid = spread_offsets(along_offsets, row_count)
    scores = (
        jnp.einsum("qhd,khd->hqk", query_rows, key_rows, preferred_element_type=jnp.float32)
        / math.sqrt(depth)
        + bias_grid
    )
    query_pos = q_start + jnp.arange(row_count, dtype=jnp.int32)
    key_pos = jnp.arange(key_count, dtype=jnp.int32)
    allowed = key_pos[None, :] // BLK <= query_pos[:, None] // BLK
    return (jnp.where(allowed[None], scores, masked_score), picks_table)


def general_device(
    tokens, expert_ids, gain_attn, w_qkv, w_out, rel_bias, gain_ffn, router, w_in, w_down, cotangent
):
    shard_list = (gain_attn, w_qkv, w_out, rel_bias, gain_ffn, router, w_in, w_down)
    (
        gain_first,
        qkv_weight,
        out_weight,
        bias_table,
        gain_second,
        route_weight,
        inner_weight,
        outer_weight,
    ) = (
        lax.all_gather(shard_list[0], "gx", axis=0, tiled=True),
        lax.all_gather(shard_list[1], "gx", axis=1, tiled=True),
        lax.all_gather(shard_list[2], "gx", axis=1, tiled=True),
        lax.all_gather(shard_list[3], "gx", axis=0, tiled=True),
        lax.all_gather(shard_list[4], "gx", axis=0, tiled=True),
        lax.all_gather(shard_list[5], "gx", axis=0, tiled=True),
        lax.all_gather(shard_list[6], "gx", axis=1, tiled=True),
        lax.all_gather(shard_list[7], "gx", axis=2, tiled=True),
    )
    tok_dev = tokens.shape[0]
    count_x = lax.axis_size("gx")
    count_y = lax.axis_size("gy")
    total_tokens = tok_dev * count_x * count_y
    model_width = tokens.shape[1]
    expert_count = route_weight.shape[1]
    top_count = expert_ids.shape[1]
    local_experts = inner_weight.shape[0]
    head_count = bias_table.shape[1]
    head_width = qkv_weight.shape[2]
    depth = head_width // head_count
    q_rows = min(512, LEN)
    per_seq = LEN // q_rows
    inputs_float = tokens.astype(jnp.float32)
    normed_one, scale_one = normalize(inputs_float)
    first_norm = (normed_one * gain_first.astype(jnp.float32)).astype(jnp.bfloat16)
    group_rows = lax.all_gather(first_norm, "gy", axis=0, tiled=True)
    tok_group = group_rows.shape[0]
    seq_count = tok_group // LEN
    projected = jnp.einsum(
        "td,cdf->tcf", group_rows, qkv_weight, preferred_element_type=jnp.float32
    ).astype(jnp.bfloat16)
    projected = projected.reshape(tok_group, 3, head_count, depth)
    table_float = bias_table.astype(jnp.float32)

    def forward_block(item_index):
        seq_index = item_index // per_seq
        q_start = item_index % per_seq * q_rows
        query_rows = lax.dynamic_slice_in_dim(projected, seq_index * LEN + q_start, q_rows, 0)[:, 0]
        seq_rows = lax.dynamic_slice_in_dim(projected, seq_index * LEN, LEN, 0)
        scores, unused_picks = block_scores(query_rows, seq_rows[:, 1], table_float, q_start)
        row_max = jnp.max(scores, axis=-1, keepdims=True)
        expo_scores = jnp.exp(scores - row_max)
        row_total = jnp.sum(expo_scores, axis=-1, keepdims=True)
        soft_weights = (expo_scores / row_total).astype(jnp.bfloat16)
        block_out = jnp.einsum(
            "hqk,khd->qhd", soft_weights, seq_rows[:, 2], preferred_element_type=jnp.float32
        ).astype(jnp.bfloat16)
        return (block_out.reshape(q_rows, head_width), (row_max + jnp.log(row_total))[:, :, 0])

    attended, log_totals = lax.map(forward_block, jnp.arange(seq_count * per_seq, dtype=jnp.int32))
    attended = attended.reshape(tok_group, head_width)
    attn_sum = lax.psum_scatter(
        jnp.dot(attended, out_weight, preferred_element_type=jnp.float32).astype(jnp.bfloat16),
        "gy",
        scatter_dimension=0,
        tiled=True,
    ).astype(jnp.float32)
    hidden_state = inputs_float + attn_sum
    normed_two, scale_two = normalize(hidden_state)
    second_norm = (normed_two * gain_second.astype(jnp.float32)).astype(jnp.bfloat16)
    logits = jnp.dot(second_norm, route_weight, preferred_element_type=jnp.float32)
    route = jax.nn.softmax(logits, axis=-1)
    chosen = (
        expert_ids.reshape(-1)[:, None] == jnp.arange(expert_count, dtype=jnp.int32)[None, :]
    ).astype(jnp.int32)
    earlier = jnp.cumsum(chosen, axis=0) - chosen
    slot = jnp.sum(earlier * chosen, axis=-1).reshape(tok_dev, top_count)
    kept = (slot < CAP).astype(jnp.float32)
    counts, prob_sums = lax.psum(
        (jnp.sum(chosen, axis=0).astype(jnp.float32), jnp.sum(route, axis=0)), ("gx", "gy")
    )
    loss = expert_count * jnp.sum(counts / (total_tokens * top_count) * (prob_sums / total_tokens))
    router_load = jnp.stack(
        [
            expert_count * counts / (total_tokens * top_count),
            expert_count * prob_sums / total_tokens,
        ],
        axis=0,
    )
    slot_place = expert_ids * CAP + jnp.minimum(slot, CAP - 1)
    buffer_index = jnp.arange(expert_count * CAP, dtype=jnp.int32)[:, None, None]
    hit_table = (buffer_index == slot_place[None]).astype(jnp.float32) * kept[None]
    dispatch_matrix = jnp.sum(hit_table, axis=-1).astype(jnp.bfloat16)
    send_rows = jnp.dot(dispatch_matrix, second_norm, preferred_element_type=jnp.float32).astype(
        jnp.bfloat16
    )
    send_rows = send_rows.reshape(count_y, local_experts, CAP, model_width)
    received = lax.all_to_all(send_rows, "gy", split_axis=0, concat_axis=0, tiled=True)
    upper = jnp.einsum("slcd,ldf->slcf", received, inner_weight, preferred_element_type=jnp.float32)
    half_width = upper.shape[-1] // 2
    hidden_rows = (
        jax.nn.gelu(upper[..., :half_width], approximate=True) * upper[..., half_width:]
    ).astype(jnp.bfloat16)
    expert_out = jnp.einsum(
        "slcf,lfd->slcd", hidden_rows, outer_weight, preferred_element_type=jnp.float32
    ).astype(jnp.bfloat16)
    expert_out, upper, received = (expert_out, upper, received)
    returned = lax.all_to_all(expert_out, "gy", split_axis=0, concat_axis=0, tiled=True).reshape(
        expert_count * CAP, model_width
    )
    picked_rows = jnp.take(returned, slot_place, axis=0).astype(jnp.float32)
    gate_value = jnp.take_along_axis(route, expert_ids, axis=1) * kept
    mixed = hidden_state + jnp.sum(picked_rows * gate_value[:, :, None], axis=1)
    (
        gain_first,
        qkv_weight,
        out_weight,
        bias_table,
        gain_second,
        route_weight,
        inner_weight,
        outer_weight,
    ) = (
        lax.all_gather(shard_list[0], "gx", axis=0, tiled=True),
        lax.all_gather(shard_list[1], "gx", axis=1, tiled=True),
        lax.all_gather(shard_list[2], "gx", axis=1, tiled=True),
        lax.all_gather(shard_list[3], "gx", axis=0, tiled=True),
        lax.all_gather(shard_list[4], "gx", axis=0, tiled=True),
        lax.all_gather(shard_list[5], "gx", axis=0, tiled=True),
        lax.all_gather(shard_list[6], "gx", axis=1, tiled=True),
        lax.all_gather(shard_list[7], "gx", axis=2, tiled=True),
    )
    table_float = bias_table.astype(jnp.float32)
    grad_mixed = cotangent.astype(jnp.float32)
    grad_gate = kept * jnp.sum(grad_mixed[:, None, :] * picked_rows, axis=-1)
    gate_matrix = jnp.sum(hit_table * gate_value[None], axis=-1)
    grad_buffer = jnp.dot(gate_matrix, grad_mixed, precision=lax.Precision.HIGHEST).astype(
        jnp.bfloat16
    )
    grad_expert = lax.all_to_all(
        grad_buffer.reshape(count_y, local_experts, CAP, model_width),
        "gy",
        split_axis=0,
        concat_axis=0,
        tiled=True,
    )
    half_width = upper.shape[-1] // 2
    activated, pull_gelu = jax.vjp(
        lambda gate_part, up_part: jax.nn.gelu(gate_part, approximate=True) * up_part,
        upper[..., :half_width],
        upper[..., half_width:],
    )
    hidden_rows = activated.astype(jnp.bfloat16)
    grad_hidden = jnp.einsum(
        "slcd,lfd->slcf", grad_expert, outer_weight, preferred_element_type=jnp.float32
    )
    grad_outer = jnp.einsum(
        "slcf,slcd->lfd", hidden_rows, grad_expert, preferred_element_type=jnp.float32
    )
    grad_gate_part, grad_up_part = pull_gelu(grad_hidden)
    grad_upper = jnp.concatenate([grad_gate_part, grad_up_part], axis=-1).astype(jnp.bfloat16)
    grad_inner = jnp.einsum(
        "slcd,slcf->ldf", received, grad_upper, preferred_element_type=jnp.float32
    )
    grad_received = jnp.einsum(
        "slcf,ldf->slcd", grad_upper, inner_weight, preferred_element_type=jnp.float32
    ).astype(jnp.bfloat16)
    grad_copies = lax.all_to_all(
        grad_received, "gy", split_axis=0, concat_axis=0, tiled=True
    ).reshape(expert_count * CAP, model_width)
    grad_second = jnp.sum(
        jnp.take(grad_copies, slot_place, axis=0).astype(jnp.float32) * kept[:, :, None], axis=1
    )
    expert_hits = (expert_ids[:, :, None] == jnp.arange(expert_count, dtype=jnp.int32)).astype(
        jnp.float32
    )
    grad_route = (
        jnp.sum(grad_gate[:, :, None] * expert_hits, axis=1)
        + loss_weight * expert_count * (counts / (total_tokens * top_count)) / total_tokens
    )
    grad_logits = (
        route * (grad_route - jnp.sum(route * grad_route, axis=-1, keepdims=True))
    ).astype(jnp.bfloat16)
    grad_router = jnp.dot(second_norm.T, grad_logits, preferred_element_type=jnp.float32)
    grad_second = grad_second + jnp.dot(
        grad_logits, route_weight.T, preferred_element_type=jnp.float32
    )
    grad_hidden_state, grad_gain_second = norm_back(
        grad_second, normed_two, scale_two, gain_second.astype(jnp.float32)
    )
    grad_hidden_state = grad_mixed + grad_hidden_state
    piece_rows = lax.all_gather(grad_hidden_state.astype(jnp.bfloat16), "gy", axis=0, tiled=True)
    grad_out_weight = jnp.einsum(
        "tf,td->fd", attended, piece_rows, preferred_element_type=jnp.float32
    )
    update_rows = jnp.dot(piece_rows, out_weight.T, preferred_element_type=jnp.float32).astype(
        jnp.bfloat16
    )
    grad_out_weight, grad_attended = (grad_out_weight, update_rows)

    def backward_sequence(seq_index):
        seq_rows = lax.dynamic_slice_in_dim(projected, seq_index * LEN, LEN, 0)
        key_rows = seq_rows[:, 1]
        value_rows = seq_rows[:, 2]
        grad_keys = jnp.zeros((LEN, head_count, depth), jnp.float32)
        grad_values = jnp.zeros((LEN, head_count, depth), jnp.float32)
        grad_table = jnp.zeros(table_float.shape, jnp.float32)
        grad_queries = []
        for block_index in range(per_seq):
            q_start = block_index * q_rows
            query_rows = seq_rows[q_start : q_start + q_rows, 0]
            grad_out = lax.dynamic_slice_in_dim(
                grad_attended, seq_index * LEN + q_start, q_rows, 0
            ).reshape(q_rows, head_count, depth)
            scores, picks_table = block_scores(query_rows, key_rows, table_float, q_start)
            block_lse = log_totals[seq_index * per_seq + block_index]
            soft_probs = jnp.exp(scores - block_lse[:, :, None])
            grad_probs = jnp.einsum(
                "qhd,khd->hqk", grad_out, value_rows, preferred_element_type=jnp.float32
            )
            grad_scores = (
                soft_probs * (grad_probs - jnp.sum(soft_probs * grad_probs, axis=-1, keepdims=True))
            ).astype(jnp.bfloat16)
            grad_queries.append(
                jnp.einsum(
                    "hqk,khd->qhd", grad_scores, key_rows, preferred_element_type=jnp.float32
                )
                / math.sqrt(depth)
            )
            grad_keys = grad_keys + jnp.einsum(
                "hqk,qhd->khd", grad_scores, query_rows, preferred_element_type=jnp.float32
            ) / math.sqrt(depth)
            grad_values = grad_values + jnp.einsum(
                "hqk,qhd->khd",
                soft_probs.astype(jnp.bfloat16),
                grad_out,
                preferred_element_type=jnp.float32,
            )
            along_grads = gather_offsets(grad_scores.astype(jnp.float32), q_rows)
            grad_table = grad_table + jnp.dot(
                picks_table.T, along_grads.T, precision=lax.Precision.HIGHEST
            )
        stacked = jnp.stack(
            [jnp.concatenate(grad_queries, axis=0), grad_keys, grad_values], axis=1
        ).astype(jnp.bfloat16)
        return (stacked, grad_table)

    grad_projected, table_parts = lax.map(backward_sequence, jnp.arange(seq_count, dtype=jnp.int32))
    grad_projected = grad_projected.reshape(tok_group, 3, head_width)
    grad_bias_table = jnp.sum(table_parts, axis=0)
    grad_qkv_weight = jnp.einsum(
        "td,tcf->cdf", group_rows, grad_projected, preferred_element_type=jnp.float32
    )
    grad_slice = lax.slice_in_dim(grad_projected, 0, tok_dev * lax.axis_size("gy"), axis=0)
    grad_first = lax.psum_scatter(
        jnp.einsum(
            "tcf,cdf->td", grad_slice, qkv_weight, preferred_element_type=jnp.float32
        ).astype(jnp.bfloat16),
        "gy",
        scatter_dimension=0,
        tiled=True,
    ).astype(jnp.float32)
    grad_inputs, grad_gain_first = norm_back(
        grad_first, normed_one, scale_one, gain_first.astype(jnp.float32)
    )
    grad_tokens = grad_hidden_state + grad_inputs
    grad_gain_first, grad_gain_second, grad_router = (
        lax.psum(grad_gain_first.astype(jnp.bfloat16), "gy").astype(jnp.float32),
        lax.psum(grad_gain_second.astype(jnp.bfloat16), "gy").astype(jnp.float32),
        lax.psum(grad_router.astype(jnp.bfloat16), "gy").astype(jnp.float32),
    )
    summed_grads = (
        lax.psum_scatter(
            grad_gain_first.astype(jnp.bfloat16), "gx", scatter_dimension=0, tiled=True
        ).astype(jnp.float32),
        lax.psum_scatter(
            grad_qkv_weight.astype(jnp.bfloat16), "gx", scatter_dimension=1, tiled=True
        ).astype(jnp.float32),
        lax.psum_scatter(
            grad_out_weight.astype(jnp.bfloat16), "gx", scatter_dimension=1, tiled=True
        ).astype(jnp.float32),
        lax.psum_scatter(
            grad_bias_table.astype(jnp.bfloat16), "gx", scatter_dimension=0, tiled=True
        ).astype(jnp.float32),
        lax.psum_scatter(
            grad_gain_second.astype(jnp.bfloat16), "gx", scatter_dimension=0, tiled=True
        ).astype(jnp.float32),
        lax.psum_scatter(
            grad_router.astype(jnp.bfloat16), "gx", scatter_dimension=0, tiled=True
        ).astype(jnp.float32),
        lax.psum_scatter(
            grad_inner.astype(jnp.bfloat16), "gx", scatter_dimension=1, tiled=True
        ).astype(jnp.float32),
        lax.psum_scatter(
            grad_outer.astype(jnp.bfloat16), "gx", scatter_dimension=2, tiled=True
        ).astype(jnp.float32),
    )
    return (
        mixed.astype(jnp.bfloat16),
        loss,
        router_load,
        grad_tokens,
        summed_grads[0],
        summed_grads[1],
        summed_grads[2],
        summed_grads[3],
        summed_grads[4],
        summed_grads[5],
        summed_grads[6],
        summed_grads[7],
    )


def dot_nn(a, b):
    return lax.dot_general(a, b, (((1,), (0,)), ((), ())), preferred_element_type=jnp.float32)

def dot_nt(a, b):
    return lax.dot_general(a, b, (((1,), (1,)), ((), ())), preferred_element_type=jnp.float32)

def span_buckets():
    k = jnp.arange(2 * BLK, dtype=jnp.int32)
    return jnp.stack([bucket_of(BLK - k - BLK * d) for d in range(2)])

def attend_fwd_kernel(proj_ref, span_ref, out_ref, lse_ref, tile_ref):
    length = proj_ref.shape[1]
    blocks = length // BLK
    depth = 64
    lane = lax.broadcasted_iota(jnp.int32, (1, 2 * depth), 1)
    for h in range(2):
        for d in range(2):
            row = span_ref[h, d:d + 1, :]
            wide = jnp.broadcast_to(row, (BLK, 2 * BLK))
            turned = pltpu.roll(wide, 0, 1, stride=1, stride_axis=0)
            tile_ref[h, d] = turned[:, BLK:]
    far = [span_ref[h, 1:2, 2 * BLK - 1:2 * BLK] for h in range(2)]
    keys = proj_ref[1]
    values_t = proj_ref[2].T
    for block in range(blocks):
        rows = pl.ds(block * BLK, BLK)
        query = proj_ref[0, rows, :] * jnp.bfloat16(0.125)
        key_count = (block + 1) * BLK
        outs = []
        for h in range(2):
            picked = jnp.where((lane // depth) == h, query, jnp.bfloat16(0))
            scores = dot_nt(keys[:key_count], picked)
            parts = []
            for kb in range(block + 1):
                part = scores[kb * BLK:(kb + 1) * BLK]
                d = block - kb
                parts.append(part + (tile_ref[h, d] if d < 2 else far[h]))
            top = functools.reduce(jnp.maximum, [jnp.max(p, axis=0, keepdims=True) for p in parts])
            parts = [jnp.exp(p - top) for p in parts]
            total = functools.reduce(jnp.add, [jnp.sum(p, axis=0, keepdims=True) for p in parts])
            scale = 1.0 / total
            weights = jnp.concatenate([(p * scale).astype(jnp.bfloat16) for p in parts], axis=0)
            outs.append(dot_nn(values_t[h * depth:(h + 1) * depth, :key_count], weights))
            lse_ref[0, h:h + 1, rows] = top + jnp.log(total)
        out_ref[rows, :] = jnp.concatenate(outs, axis=0).T.astype(jnp.bfloat16)

def attend_fwd(proj, spans):
    _, length, width = proj.shape
    pairs = width // 128
    return pl.pallas_call(
        attend_fwd_kernel,
        grid=(pairs,),
        out_shape=(
            jax.ShapeDtypeStruct((length, width), jnp.bfloat16),
            jax.ShapeDtypeStruct((pairs, 2, length), jnp.float32),
            jax.ShapeDtypeStruct((2 * pairs, 2, BLK, BLK), jnp.float32),
        ),
        in_specs=[
            pl.BlockSpec((3, length, 128), lambda p: (0, 0, p)),
            pl.BlockSpec((2, 2, 2 * BLK), lambda p: (p, 0, 0)),
        ],
        out_specs=(
            pl.BlockSpec((length, 128), lambda p: (0, p)),
            pl.BlockSpec((1, 2, length), lambda p: (p, 0, 0)),
            pl.BlockSpec((2, 2, BLK, BLK), lambda p: (p, 0, 0, 0)),
        ),
        compiler_params=pltpu.CompilerParams(vmem_limit_bytes=48 * 2**20),
        name="attend_forward",
    )(proj, spans)

def attend_bwd_kernel(proj_ref, dout_ref, lse_ref, tile_ref, far_ref, dproj_ref, span_ref, dk_ref, dv_ref, near_ref):
    length = proj_ref.shape[1]
    blocks = length // BLK
    depth = 64
    lane = lax.broadcasted_iota(jnp.int32, (1, 2 * depth), 1)
    keys = proj_ref[1]
    values = proj_ref[2]
    keys_t = keys.T
    dk_ref[...] = jnp.zeros_like(dk_ref)
    dv_ref[...] = jnp.zeros_like(dv_ref)
    near_ref[...] = jnp.zeros_like(near_ref)
    far_sum = [jnp.zeros((1, BLK), jnp.float32) for h in range(2)]
    for block in range(blocks):
        rows = pl.ds(block * BLK, BLK)
        key_count = (block + 1) * BLK
        query = proj_ref[0, rows, :] * jnp.bfloat16(0.125)
        grad = dout_ref[rows, :]
        dq_parts = []
        dk_sum = None
        dv_sum = None
        for h in range(2):
            own = (lane // depth) == h
            query_h = jnp.where(own, query, jnp.bfloat16(0))
            grad_h = jnp.where(own, grad, jnp.bfloat16(0))
            scores = dot_nt(keys[:key_count], query_h)
            grad_p = dot_nt(values[:key_count], grad_h)
            lse = lse_ref[0, h:h + 1, rows]
            far = far_ref[0, h:h + 1, 0:1]
            probs = []
            delta = None
            for kb in range(block + 1):
                d = block - kb
                part = scores[kb * BLK:(kb + 1) * BLK]
                part = jnp.exp(part + ((tile_ref[h, d] - lse) if d < 2 else (far - lse)))
                probs.append(part)
                term = jnp.sum(part * grad_p[kb * BLK:(kb + 1) * BLK], axis=0, keepdims=True)
                delta = term if delta is None else delta + term
            ds = []
            for kb in range(block + 1):
                d = block - kb
                part = probs[kb] * (grad_p[kb * BLK:(kb + 1) * BLK] - delta)
                if d < 2:
                    near_ref[h, d] += part
                else:
                    far_sum[h] = far_sum[h] + jnp.sum(part, axis=0, keepdims=True)
                ds.append(part.astype(jnp.bfloat16))
            ds = jnp.concatenate(ds, axis=0)
            weights = jnp.concatenate([p.astype(jnp.bfloat16) for p in probs], axis=0)
            dv_h = dot_nn(weights, grad_h)
            dk_h = dot_nn(ds, query_h)
            dv_sum = dv_h if dv_sum is None else dv_sum + dv_h
            dk_sum = dk_h if dk_sum is None else dk_sum + dk_h
            dq_parts.append(dot_nn(keys_t[h * depth:(h + 1) * depth, :key_count], ds))
        dk_ref[:key_count] += dk_sum
        dv_ref[:key_count] += dv_sum
        dproj_ref[0, rows, :] = (jnp.concatenate(dq_parts, axis=0).T * 0.125).astype(jnp.bfloat16)
    dproj_ref[1] = dk_ref[...].astype(jnp.bfloat16)
    dproj_ref[2] = dv_ref[...].astype(jnp.bfloat16)
    flip = (
        lax.broadcasted_iota(jnp.int32, (BLK, BLK), 0) + lax.broadcasted_iota(jnp.int32, (BLK, BLK), 1) == BLK - 1
    ).astype(jnp.bfloat16)
    for h in range(2):
        for d in range(2):
            near = near_ref[h, d]
            near_high = near.astype(jnp.bfloat16)
            near_low = (near - near_high.astype(jnp.float32)).astype(jnp.bfloat16)
            flipped = dot_nn(flip, near_high) + dot_nn(flip, near_low)
            wide = jnp.concatenate([flipped, jnp.zeros((BLK, BLK), jnp.float32)], axis=1)
            turned = pltpu.roll(wide, 1, 1, stride=1, stride_axis=0)
            span_ref[h, d:d + 1, :] = jnp.sum(turned, axis=0, keepdims=True)
        lanes = lax.broadcasted_iota(jnp.int32, (1, 2 * BLK), 1)
        total = jnp.sum(far_sum[h], axis=1, keepdims=True)
        span_ref[h, 1:2, :] += jnp.where(lanes == 2 * BLK - 1, total, 0.0)

def attend_bwd(proj, dout, lse, tiles, far):
    _, length, width = proj.shape
    pairs = width // 128
    return pl.pallas_call(
        attend_bwd_kernel,
        grid=(pairs,),
        out_shape=(
            jax.ShapeDtypeStruct((3, length, width), jnp.bfloat16),
            jax.ShapeDtypeStruct((2 * pairs, 2, 2 * BLK), jnp.float32),
        ),
        in_specs=[
            pl.BlockSpec((3, length, 128), lambda p: (0, 0, p)),
            pl.BlockSpec((length, 128), lambda p: (0, p)),
            pl.BlockSpec((1, 2, length), lambda p: (p, 0, 0)),
            pl.BlockSpec((2, 2, BLK, BLK), lambda p: (p, 0, 0, 0)),
            pl.BlockSpec((1, 2, 128), lambda p: (p, 0, 0)),
        ],
        out_specs=(
            pl.BlockSpec((3, length, 128), lambda p: (0, 0, p)),
            pl.BlockSpec((2, 2, 2 * BLK), lambda p: (p, 0, 0)),
        ),
        scratch_shapes=[
            pltpu.VMEM((length, 128), jnp.float32),
            pltpu.VMEM((length, 128), jnp.float32),
            pltpu.VMEM((2, 2, BLK, BLK), jnp.float32),
        ],
        compiler_params=pltpu.CompilerParams(vmem_limit_bytes=48 * 2**20),
        name="attend_backward",
    )(proj, dout, lse, tiles, far)


AXES = ("gx", "gy")
MESH_ID = pl.DeviceIdType.MESH


def fits_fast(mesh):
    return mesh.shape["gx"] == 8 and mesh.shape["gy"] == 4


def places():
    x = lax.axis_index("gx")
    z = lax.axis_index("gy")
    core = x % 2
    chip = x // 2
    along_z = (z + 1 - 2 * (z % 2), (z + 2) % 4, 3 - z)
    chips = (chip + 1 - 2 * (chip % 2), (chip + 2) % 4, 3 - chip)
    return x, z, along_z, tuple(2 * other + core for other in chips), x + 1 - 2 * core


def gather_kernel(
    tok_ref, wq_ref, wo_ref, small_ref, seq_ref, wqs_ref, wos_ref, smalls_ref, send_sem, recv_sem, local_sem
):
    x, z, along_z, across, sibling = places()
    peers = [(x, other) for other in along_z] + [(other, z) for other in across] + [(sibling, z)]
    barrier = pltpu.get_barrier_semaphore()
    for peer in peers:
        pl.semaphore_signal(barrier, inc=1, device_id=peer, device_id_type=MESH_ID)
    pl.semaphore_wait(barrier, len(peers))
    started = []

    def send(source, target, device):
        index = len(started)
        copy = pltpu.make_async_remote_copy(
            src_ref=source,
            dst_ref=target,
            send_sem=send_sem.at[index],
            recv_sem=recv_sem.at[index],
            device_id=device,
            device_id_type=MESH_ID,
        )
        copy.start()
        started.append(copy)
        return copy

    depth = wq_ref.shape[1]
    width = wq_ref.shape[2]
    rows_out = wo_ref.shape[0]

    def qkv_part(owner, slot):
        return wqs_ref.at[:, pl.ds(pl.multiple_of(owner * depth, depth), depth), pl.ds(slot * width, width)]

    def out_part(owner, slot, slots):
        return wos_ref.at[
            pl.ds(slot * rows_out, slots * rows_out), pl.ds(pl.multiple_of(owner * depth, depth), depth)
        ]

    out_slots = (2, 1, 3)
    locals_started = []

    def keep(source, target):
        copy = pltpu.make_async_copy(source, target, local_sem.at[len(locals_started)])
        copy.start()
        locals_started.append(copy)
        return copy

    half = z % 2
    kept_wq = keep(wq_ref, qkv_part(x, 0))
    kept_wo = keep(wo_ref, out_part(x, 0, 1))
    kept_small = keep(small_ref, smalls_ref.at[0, x])
    keep(tok_ref, seq_ref.at[half])
    small_z = [send(small_ref, smalls_ref.at[j + 1, x], (x, along_z[j])) for j in range(3)]
    wq_z = send(wq_ref, qkv_part(x, 1), (x, along_z[1]))
    wo_z = [send(wo_ref, out_part(x, out_slots[j], 1), (x, along_z[j])) for j in range(3)]
    wq_first = [send(wq_ref, qkv_part(x, 0), (other, z)) for other in across + (sibling,)]
    send(tok_ref, seq_ref.at[half], (x, along_z[0]))
    kept_small.wait()
    for copy in small_z:
        copy.wait_recv()
    small_x = [send(smalls_ref.at[:, x], smalls_ref.at[:, x], (other, z)) for other in across + (sibling,)]
    wq_z.wait_recv()
    wq_second = [send(qkv_part(x, 1), qkv_part(x, 1), (other, z)) for other in across + (sibling,)]
    kept_wo.wait()
    for copy in wo_z:
        copy.wait_recv()
    wo_x = [send(out_part(x, 0, 4), out_part(x, 0, 4), (other, z)) for other in across + (sibling,)]
    waited = small_z + [wq_z] + wo_z
    for j in range(3):
        owner = across[j]
        small_x[j].wait_recv()
        send(smalls_ref.at[:, owner], smalls_ref.at[:, owner], (sibling, z))
        wq_first[j].wait_recv()
        send(qkv_part(owner, 0), qkv_part(owner, 0), (sibling, z))
        waited += [small_x[j], wq_first[j]]
    for j in range(3):
        owner = across[j]
        wq_second[j].wait_recv()
        send(qkv_part(owner, 1), qkv_part(owner, 1), (sibling, z))
        wo_x[j].wait_recv()
        send(out_part(owner, 0, 4), out_part(owner, 0, 4), (sibling, z))
        waited += [wq_second[j], wo_x[j]]
    for copy in started:
        if not any(copy is other for other in waited):
            copy.wait_recv()
    for copy in started:
        copy.wait_send()
    kept_wq.wait()
    locals_started[3].wait()


def gather_params(tokens, w_qkv, w_out, small):
    tok_dev, model_width = tokens.shape
    copies = 3 + 1 + 3 + 4 + 1 + 4 + 4 + 4 + 12
    anywhere = pl.BlockSpec(memory_space=pl.ANY)
    return pl.pallas_call(
        gather_kernel,
        out_shape=(
            jax.ShapeDtypeStruct((2, tok_dev, model_width), jnp.bfloat16),
            jax.ShapeDtypeStruct((3, model_width, 2 * w_qkv.shape[2]), jnp.bfloat16),
            jax.ShapeDtypeStruct((4 * w_out.shape[0], model_width), jnp.bfloat16),
            jax.ShapeDtypeStruct((4, 8) + small.shape, jnp.bfloat16),
        ),
        in_specs=[anywhere] * 4,
        out_specs=(anywhere,) * 4,
        scratch_shapes=[
            pltpu.SemaphoreType.DMA((copies,)),
            pltpu.SemaphoreType.DMA((copies,)),
            pltpu.SemaphoreType.DMA((4,)),
        ],
        compiler_params=pltpu.CompilerParams(collective_id=0, has_side_effects=True),
        name="gather_params",
    )(tokens, w_qkv, w_out, small)


def swap_z(values, step):
    return lax.ppermute(values, "gy", [(i, i ^ step) for i in range(4)])


def swap_core(values):
    return lax.ppermute(values, "gx", [(i, i ^ 1) for i in range(8)])


def exchange_slots(rows):
    groups = [[(2 * c + h) * 4 + z for c in range(4) for z in range(4)] for h in range(2)]
    return lax.all_to_all(rows, AXES, 0, 0, axis_index_groups=groups, tiled=True)


def geglu(gate_part, up_part):
    return jax.nn.gelu(gate_part, approximate=True) * up_part


def fast_device(
    tokens, expert_ids, gain_attn, w_qkv, w_out, rel_bias, gain_ffn, router, w_in, w_down, cotangent
):
    f32, bf16 = jnp.float32, jnp.bfloat16
    z = lax.axis_index("gy")
    half = z % 2
    tok_dev, model_width = tokens.shape
    total_tokens = tok_dev * 32
    expert_count = router.shape[1]
    top_count = expert_ids.shape[1]
    shard = model_width // 8
    local_experts, _, upper_width = w_in.shape
    quarter = upper_width // 4
    bucket_count = rel_bias.shape[0] * 8
    group_heads = rel_bias.shape[1]

    expert_row = jnp.arange(expert_count, dtype=jnp.int32)
    hits = [(expert_ids[:, c][:, None] == expert_row[None]) for c in range(top_count)]
    both = sum(hit.astype(bf16) for hit in hits)
    steps = jnp.arange(tok_dev, dtype=jnp.int32)
    lower = (steps[None, :] < steps[:, None]).astype(bf16)
    before = jnp.dot(lower, both, preferred_element_type=f32)
    slots = [jnp.sum(jnp.where(hit, before, 0.0), axis=1).astype(jnp.int32) for hit in hits]
    kept = [slot < CAP for slot in slots]
    local_counts = jnp.sum(both.astype(f32), axis=0)
    count_high = jnp.floor(local_counts / 32.0)
    count_low = local_counts - 32.0 * count_high

    def lanes(rows):
        return jnp.pad(rows.astype(bf16), ((0, 0), (0, shard - rows.shape[1])))

    small = jnp.concatenate(
        [
            router.T,
            gain_attn[None],
            gain_ffn[None],
            lanes(rel_bias),
            lanes(count_high[None]),
            lanes(count_low[None]),
            jnp.zeros((8, shard), bf16),
        ],
        axis=0,
    )
    seq_tokens, qkv_weight, out_weight, smalls = gather_params(tokens, w_qkv, w_out, small)

    inner_sent = (
        w_in.reshape(local_experts, shard, 2, 2, quarter).transpose(0, 3, 1, 2, 4).reshape(8, shard, 2 * quarter)
    )
    outer_sent = w_down.reshape(8, quarter, shard)
    outer_own = lax.all_to_all(outer_sent, "gx", 0, 0, tiled=True)
    outer_own = outer_own.transpose(1, 0, 2).reshape(quarter, model_width)
    inner_own = lax.all_to_all(inner_sent, "gx", 0, 0, tiled=True).reshape(model_width, 2 * quarter)
    outer_parts = (outer_own, swap_core(outer_own))
    inner_parts = (inner_own, swap_core(inner_own))

    own_small = smalls[0]
    router_t = own_small[:, :16].transpose(1, 0, 2).reshape(expert_count, model_width)
    gain_first = own_small[:, 16].reshape(model_width).astype(f32)
    gain_second = own_small[:, 17].reshape(model_width).astype(f32)
    bias_table = jnp.concatenate(
        [smalls[j, :, 18:22, :group_heads].reshape(bucket_count, group_heads) for j in (0, 2)], axis=1
    )
    all_counts = smalls[:, :, 22:24, :expert_count].astype(f32).sum(axis=(0, 1))
    counts = 32.0 * all_counts[0] + all_counts[1]

    seq_float = seq_tokens.reshape(2 * tok_dev, model_width).astype(f32)
    seq_normed, _ = normalize(seq_float)
    first_norm = (seq_normed * gain_first).astype(bf16)
    projected = jnp.einsum("td,cdf->ctf", first_norm, qkv_weight, preferred_element_type=f32).astype(bf16)
    picks = (span_buckets().reshape(-1)[:, None] == jnp.arange(bucket_count, dtype=jnp.int32)).astype(bf16)
    spans = jnp.einsum("kb,bh->hk", picks, bias_table, preferred_element_type=f32)
    head_count = spans.shape[0]
    spans = spans.reshape(head_count, 2, 2 * BLK)
    attended, log_totals, bias_tiles = attend_fwd(projected, spans)
    attended = attended.reshape(2, tok_dev, -1)
    attended_other = swap_z(lax.dynamic_index_in_dim(attended, 1 - half, 0, keepdims=False), 1)
    attended = jnp.concatenate(
        [lax.dynamic_index_in_dim(attended, half, 0, keepdims=False), attended_other], axis=1
    )
    inputs_float = tokens.astype(f32)
    hidden_state = inputs_float + jnp.dot(attended, out_weight, preferred_element_type=f32)
    normed_two, scale_two = normalize(hidden_state)
    second_norm = (normed_two * gain_second).astype(bf16)
    logits = lax.dot_general(second_norm, router_t, (((1,), (1,)), ((), ())), preferred_element_type=f32)
    route = jax.nn.softmax(logits, axis=-1)

    gates = [
        jnp.where(keep, jnp.sum(jnp.where(hit, route, 0.0), axis=1), 0.0) for hit, keep in zip(hits, kept)
    ]
    spots = [
        jnp.where(keep, ((expert_ids[:, c] % 4) * 4 + expert_ids[:, c] // 4) * CAP + slots[c], -1)
        for c, keep in enumerate(kept)
    ]
    buffer_rows = jnp.arange(expert_count * CAP, dtype=jnp.int32)
    marks = [buffer_rows[:, None] == spot[None] for spot in spots]
    dispatch = (marks[0] | marks[1]).astype(bf16)
    gate_rows = jnp.sum(
        jnp.where(marks[0], gates[0][None], 0.0) + jnp.where(marks[1], gates[1][None], 0.0), axis=1
    )
    send_rows = jnp.dot(dispatch, second_norm, preferred_element_type=f32).astype(bf16)
    received = exchange_slots(send_rows.reshape(expert_count, CAP, model_width)).reshape(-1, model_width)
    grad_rows = (jnp.dot(dispatch, cotangent, preferred_element_type=f32) * gate_rows[:, None]).astype(bf16)
    grad_expert = exchange_slots(grad_rows.reshape(expert_count, CAP, model_width)).reshape(-1, model_width)

    uppers = [jnp.dot(received, part, preferred_element_type=f32) for part in inner_parts]
    hiddens = [geglu(upper[:, :quarter], upper[:, quarter:]).astype(bf16) for upper in uppers]
    expert_out = sum(
        jnp.dot(hidden, part, preferred_element_type=f32) for hidden, part in zip(hiddens, outer_parts)
    ).astype(bf16)
    returned = exchange_slots(expert_out.reshape(expert_count, CAP, model_width)).reshape(-1, model_width)

    grad_uppers = []
    for upper, part in zip(uppers, outer_parts):
        grad_hidden = lax.dot_general(grad_expert, part, (((1,), (1,)), ((), ())), preferred_element_type=f32)
        _, pull_back = jax.vjp(geglu, upper[:, :quarter], upper[:, quarter:])
        grad_uppers.append(jnp.concatenate(pull_back(grad_hidden), axis=1).astype(bf16))
    grad_received = sum(
        lax.dot_general(grad_upper, part, (((1,), (1,)), ((), ())), preferred_element_type=f32)
        for grad_upper, part in zip(grad_uppers, inner_parts)
    ).astype(bf16)
    grad_copies = exchange_slots(grad_received.reshape(expert_count, CAP, model_width)).reshape(-1, model_width)

    def over_rows(left, right):
        return lax.dot_general(left, right, (((0,), (0,)), ((), ())), preferred_element_type=f32)

    grad_inner_other = swap_core(over_rows(received, grad_uppers[1]).astype(bf16))
    grad_outer_other = swap_core(over_rows(hiddens[1], grad_expert).astype(bf16))
    grad_inner = (over_rows(received, grad_uppers[0]) + grad_inner_other.astype(f32)).astype(bf16)
    grad_outer = (over_rows(hiddens[0], grad_expert) + grad_outer_other.astype(f32)).astype(bf16)
    grad_inner = lax.all_to_all(grad_inner.reshape(8, shard, 2 * quarter), "gx", 0, 0, tiled=True)
    grad_inner = (
        grad_inner.reshape(local_experts, 2, shard, 2, quarter)
        .transpose(0, 2, 3, 1, 4)
        .reshape(local_experts, shard, upper_width)
        .astype(f32)
    )
    grad_outer = lax.all_to_all(
        grad_outer.reshape(quarter, 8, shard).transpose(1, 0, 2), "gx", 0, 0, tiled=True
    )
    grad_outer = grad_outer.reshape(local_experts, 2 * quarter, shard).astype(f32)

    picked = [
        lax.dot_general(mark.astype(bf16), returned, (((0,), (0,)), ((), ())), preferred_element_type=f32)
        for mark in marks
    ]
    mixed = hidden_state + (picked[0] * gates[0][:, None] + picked[1] * gates[1][:, None])
    grad_mixed = cotangent.astype(f32)
    grad_gates = [jnp.sum(grad_mixed * rows, axis=1) for rows in picked]
    grad_second = over_rows(dispatch, grad_copies)
    grad_route = sum(
        jnp.where(hit, grad_gate[:, None], 0.0) for hit, grad_gate in zip(hits, grad_gates)
    ) + loss_weight * expert_count * (counts / (total_tokens * top_count)) / total_tokens
    grad_logits = (
        route * (grad_route - jnp.sum(route * grad_route, axis=-1, keepdims=True))
    ).astype(bf16)
    grad_router_t = over_rows(grad_logits, second_norm)
    grad_second = grad_second + jnp.dot(grad_logits, router_t, preferred_element_type=f32)
    grad_hidden_state, grad_gain_second = norm_back(grad_second, normed_two, scale_two, gain_second)
    grad_hidden_state = grad_mixed + grad_hidden_state

    grad_part = grad_hidden_state.astype(bf16)
    grad_attended = lax.dot_general(
        grad_part, out_weight, (((1,), (1,)), ((), ())), preferred_element_type=f32
    ).astype(bf16)
    own_width = grad_attended.shape[1] // 2
    grad_own = grad_attended[:, :own_width]
    grad_other = swap_z(grad_attended[:, own_width:], 1)
    grad_seq = jnp.where(
        half == 0,
        jnp.concatenate([grad_own, grad_other], axis=0),
        jnp.concatenate([grad_other, grad_own], axis=0),
    )
    far_bias = jnp.broadcast_to(
        spans[:, 1, 2 * BLK - 1].reshape(head_count // 2, 2, 1), (head_count // 2, 2, 128)
    )
    grad_projected, grad_spans = attend_bwd(projected, grad_seq, log_totals, bias_tiles, far_bias)
    grad_out_weight = over_rows(attended, grad_part).astype(bf16)
    grad_out_weight = lax.psum_scatter(grad_out_weight, "gx", scatter_dimension=1, tiled=True)
    grad_out_weight = grad_out_weight.reshape(4, w_out.shape[0], shard)
    order = jnp.arange(4, dtype=jnp.int32) ^ z
    order = jnp.where(order == 1, 2, jnp.where(order == 2, 1, order))
    grad_out_weight = jnp.take(grad_out_weight, order, axis=0)
    grad_out_weight = lax.psum_scatter(grad_out_weight, "gy", scatter_dimension=0, tiled=True)[0].astype(f32)

    group_width = w_qkv.shape[2]
    grad_qkv = jnp.einsum("td,ctf->cdf", first_norm, grad_projected, preferred_element_type=f32).astype(bf16)
    grad_qkv = lax.psum_scatter(grad_qkv, "gx", scatter_dimension=1, tiled=True)
    grad_qkv = grad_qkv[:, :, :group_width].astype(f32) + swap_z(grad_qkv[:, :, group_width:], 2).astype(f32)

    grad_first = jnp.einsum("ctf,cdf->td", grad_projected, qkv_weight, preferred_element_type=f32)
    grad_first = grad_first.reshape(2, tok_dev, model_width)
    sent_first = lax.dynamic_index_in_dim(grad_first, 1 - half, 0, keepdims=False).astype(bf16)
    grad_first = lax.dynamic_index_in_dim(grad_first, half, 0, keepdims=False) + swap_z(sent_first, 1).astype(f32)
    normed_one, scale_one = normalize(inputs_float)
    grad_inputs, grad_gain_first = norm_back(grad_first, normed_one, scale_one, gain_first)
    grad_tokens = grad_hidden_state + grad_inputs

    grad_table = jnp.einsum(
        "hk,kb->bh", grad_spans.reshape(head_count, -1), picks.astype(f32), precision=lax.Precision.HIGHEST
    )
    grad_heads = jnp.zeros((bucket_count, 4, group_heads), f32)
    grad_heads = lax.dynamic_update_slice(grad_heads, grad_table[:, None, :group_heads], (0, z, 0))
    grad_heads = lax.dynamic_update_slice(grad_heads, grad_table[:, None, group_heads:], (0, z ^ 2, 0))
    grad_heads = grad_heads.reshape(8, bucket_count // 8, 4 * group_heads)
    route_sums = jnp.broadcast_to(jnp.sum(route, axis=0), (8, 1, expert_count))

    def wide(rows):
        return jnp.pad(rows, ((0, 0), (0, 0), (0, shard - rows.shape[2])))

    sums = jnp.concatenate(
        [
            grad_gain_first.reshape(8, 1, shard),
            grad_gain_second.reshape(8, 1, shard),
            grad_router_t.reshape(expert_count, 8, shard).transpose(1, 0, 2),
            wide(grad_heads),
            wide(route_sums),
            jnp.zeros((8, 1, shard), f32),
        ],
        axis=1,
    )
    sums = lax.psum_scatter(sums, "gx", scatter_dimension=0, tiled=True)
    sums = lax.psum(sums, "gy")[0]
    prob_sums = sums[22, :expert_count]
    loss = expert_count * jnp.sum(counts / (total_tokens * top_count) * (prob_sums / total_tokens))
    router_load = jnp.stack(
        [
            expert_count * counts / (total_tokens * top_count),
            expert_count * prob_sums / total_tokens,
        ],
        axis=0,
    )
    grad_rel_bias = lax.dynamic_slice(sums, (18, z * group_heads), (bucket_count // 8, group_heads))
    return (
        mixed.astype(bf16),
        loss,
        router_load,
        grad_tokens,
        sums[0],
        grad_qkv,
        grad_out_weight,
        grad_rel_bias,
        sums[1],
        sums[2:18].T,
        grad_inner,
        grad_outer,
    )


def solution(mesh):
    in_specs = (
        P(("gx", "gy"), None),
        P(("gx", "gy"), None),
        P("gx"),
        P(None, "gx", "gy"),
        P("gy", "gx"),
        P("gx", "gy"),
        P("gx"),
        P("gx", None),
        P("gy", "gx", None),
        P("gy", None, "gx"),
        P(("gx", "gy"), None),
    )
    out_specs = (
        P(("gx", "gy"), None),
        P(),
        P(),
        P(("gx", "gy"), None),
        P("gx"),
        P(None, "gx", "gy"),
        P("gy", "gx"),
        P("gx", "gy"),
        P("gx"),
        P("gx", None),
        P("gy", "gx", None),
        P("gy", None, "gx"),
    )
    return jax.shard_map(
        fast_device if fits_fast(mesh) else general_device, mesh=mesh, in_specs=in_specs, out_specs=out_specs, check_vma=False
    )
```

profile of v0, /device:TPU:0, one launch (start us, length us, event | category | flops | bytes accessed | tf_op | source)
XLA Modules:
  0.0 892.3 jit_solution(4692380180272401883)
XLA Ops:
  7.2 5.2 all-to-all-start.2
  12.4 8.2 copy.82
  20.6 5.7 copy.83
  26.3 21.1 %all-to-all-done.2 = bf16[8,1408,128]{2,1,0:T(8,128)(2,1)S(1)} async-done(((bf16[8,1408,128]{2,1,0:T(8,128)(2,1)}), bf16[8,1408,128]{2,1,0:T(8,128)(2,1)S(1)}, u32[]{:S(2)}, u32[]{:S(2)}) %all-to-all-start.2) | async-done | bytes 2883616 | tf_op jit(solution)/shard_map/all_to_all | solution.py:782
  47.5 4.9 all-to-all-start.1
  52.7 1.8 concatenate.26.small_ref
  54.5 95.6 %gather_params.1 = (bf16[2,512,1024]{2,1,0:T(8,128)(2,1)}, bf16[3,1024,512]{2,1,0:T(8,128)(2,1)}, bf16[1024,1024]{1,0:T(8,128)(2,1)}, bf16[4,8,32,128]{3,2,1,0:T(8,128)(2,1)}) custom-call(bf16[512,1024]{1,0:T(8,128)(2,1)} %tok_ref.1, bf16[3,128,256]{2,1,0:T(8,128)(2,1)} %wq_ref.1, bf16[256,128]{1,0:T(8,128)(2,1)} %wo_ref.1, ...), custom_call_target="tpu_custom_call" | custom-call | tf_op jit(solution)/shard_map/gather_params/pallas_call | solution.py:696
  150.1 2.1 multiply_reduce_fusion
  155.2 2.1 fusion.18
  158.7 3.7 convert_bitcast_fusion.1.proj_ref
  162.5 19.8 %attend_forward.1 = (bf16[1024,512]{1,0:T(8,128)(2,1)S(1)}, f32[4,2,1024]{2,1,0:T(2,128)S(1)}, f32[8,2,256,256]{3,2,1,0:T(8,128)}) custom-call(bf16[3,1024,512]{2,1,0:T(8,128)(2,1)S(1)} %convert_bitcast_fusion.1.proj_ref, f32[8,2,512]{2,1,0:T(2,128)S(1)} %reshape.566.span_ref), custom_call_target="tpu_custom_call" | custom-call | tf_op jit(solution)/shard_map/attend_forward/pallas_call | solution.py:458
  184.1 12.7 %collective-permute-done = bf16[512,512]{1,0:T(8,128)(2,1)S(1)} collective-permute-done((bf16[512,512]{1,0:T(8,128)(2,1)S(1)}, bf16[512,512]{1,0:T(8,128)(2,1)S(1)}, u32[]{:S(2)}, u32[]{:S(2)}) %collective-permute-start) | collective-permute-done | bytes 524320 | tf_op jit(solution)/shard_map/ppermute | solution.py:717
  200.7 3.0 convolution_convert_fusion.1
  203.7 5.2 all-to-all-start
  208.9 8.2 copy.84
  217.2 2.7 copy.85
  220.4 49.6 %all-to-all-done = bf16[16,80,1024]{2,1,0:T(8,128)(2,1)} async-done(((bf16[16,80,1024]{2,1,0:T(8,128)(2,1)}), bf16[16,80,1024]{2,1,0:T(8,128)(2,1)}, u32[]{:S(2)}, u32[]{:S(2)}) %all-to-all-start) | async-done | bytes 2621472 | tf_op jit(solution)/shard_map/all_to_all | solution.py:726
  270.0 11.2 %fusion.122 = f32[1280,2816]{1,0:T(8,128)S(1)} fusion(bf16[1280,1024]{1,0:T(8,128)(2,1)} %bitcast.18, bf16[1024,2816]{1,0:T(8,128)(2,1)} %bitcast.196), kind=kOutput, calls=%fused_computation.254 | convolution fusion | flops 7381975040 | bytes 22806528 | tf_op jit(solution)/shard_map/dot_general | solution.py:837
  281.2 3.0 multiply_convert_fusion.3
  284.2 2.8 copy-done.7
  287.0 4.3 fusion.123
  291.3 11.2 %fusion.124 = f32[1280,2816]{1,0:T(8,128)S(1)} fusion(bf16[1280,1024]{1,0:T(8,128)(2,1)} %bitcast.18, bf16[1024,2816]{1,0:T(8,128)(2,1)} %collective-permute-done.1), kind=kOutput, calls=%fused_computation.256 | convolution fusion | flops 7381975040 | bytes 22806528 | tf_op jit(solution)/shard_map/dot_general | solution.py:837
  302.5 2.6 multiply_convert_fusion.2
  305.1 2.5 copy-done.6
  309.2 5.8 add_convert_fusion.3
  314.9 4.8 all-to-all-start.3
  321.6 58.8 %all-to-all-done.3 = bf16[16,80,1024]{2,1,0:T(8,128)(2,1)} async-done(((bf16[16,80,1024]{2,1,0:T(8,128)(2,1)}), bf16[16,80,1024]{2,1,0:T(8,128)(2,1)}, u32[]{:S(2)}, u32[]{:S(2)}) %all-to-all-start.3) | async-done | bytes 2621472 | tf_op jit(solution)/shard_map/all_to_all | solution.py:726
  380.4 3.4 fusion.22
  383.8 5.5 fusion.31
  391.8 64.4 %all_to_all.40 = bf16[16,80,1024]{2,1,0:T(8,128)(2,1)S(1)} all-to-all(bf16[16,80,1024]{2,1,0:T(8,128)(2,1)S(1)} %bitcast.210), channel_id=1, replica_groups={{0,1,2,3,8,9,10,11,16,17,18,19,24,25,26,27},{4,5,6,7,12,13,14,15,20,21,..., dimensions={0} | all-to-all | bytes 5242880 | tf_op jit(solution)/shard_map/all_to_all | solution.py:726
  456.2 14.9 %fusion.6 = (bf16[1280,1408]{1,0:T(8,128)(2,1)}, bf16[1280,1408]{1,0:T(8,128)(2,1)}) fusion(f32[1280,2816]{1,0:T(8,128)} %copy-done.7, bf16[1280,1024]{1,0:T(8,128)(2,1)S(1)} %bitcast.203, bf16[1408,1024]{0,1:T(8,128)(2,1)S(1)} %bitcast.201), kind=kOutput, calls=%fused_computation.13 | convolution fusion | flops 3734241280 | bytes 27131904 | tf_op jit(solution)/shard_map/dot_general | solution.py:846
  471.1 13.2 %fusion.16 = f32[1280,1024]{1,0:T(8,128)} fusion(bf16[1024,2816]{1,0:T(8,128)(2,1)} %bitcast.197, bf16[1280,1408]{1,0:T(8,128)(2,1)} %get-tuple-element.108, bf16[1280,1408]{1,0:T(8,128)(2,1)} %get-tuple-element.107), kind=kOutput, calls=%fused_computation.36 | convolution fusion | flops 7396392960 | bytes 18219008 | tf_op jit(solution)/shard_map/dot_general | solution.py:850
  484.4 12.9 %fusion.13 = (bf16[1280,1408]{1,0:T(8,128)(2,1)}, bf16[1280,1408]{1,0:T(8,128)(2,1)}) fusion(f32[1280,2816]{1,0:T(8,128)S(1)} %bitcast.186, bf16[1280,1024]{1,0:T(8,128)(2,1)} %bitcast.204, bf16[1408,1024]{0,1:T(8,128)(2,1)} %copy-done.43), kind=kOutput, calls=%fused_computation.20 | convolution fusion | flops 3734241280 | bytes 27131904 | tf_op jit(solution)/shard_map/dot_general | solution.py:846
  497.3 13.4 %add_convert_fusion.2 = bf16[1280,1024]{1,0:T(8,128)(2,1)} fusion(f32[1280,1024]{1,0:T(8,128)} %fusion.16, bf16[1024,2816]{1,0:T(8,128)(2,1)} %collective-permute-done.1, bf16[1280,1408]{1,0:T(8,128)(2,1)} %get-tuple-element.106, bf16[1280,1408]{1,0:T(8,128)(2,1)} %get-tuple-element.105), kind=kOutput, calls=%fused_computation.31 | convolution fusion | flops 7399014400 | bytes 20840448 | tf_op jit(solution)/shard_map/dot_general | solution.py:850
  510.7 4.6 all-to-all-start.5
  516.7 59.0 %all-to-all-done.5 = bf16[16,80,1024]{2,1,0:T(8,128)(2,1)} async-done(((bf16[16,80,1024]{2,1,0:T(8,128)(2,1)}), bf16[16,80,1024]{2,1,0:T(8,128)(2,1)}, u32[]{:S(2)}, u32[]{:S(2)}) %all-to-all-start.5) | async-done | bytes 2621472 | tf_op jit(solution)/shard_map/all_to_all | solution.py:726
  575.7 3.4 fusion.35
  581.4 1.9 convert_add_fusion
  587.2 11.2 %convolution_convert_fusion = bf16[1024,2816]{1,0:T(8,128)(2,1)} fusion(bf16[1280,1024]{1,0:T(8,128)(2,1)} %bitcast.18, bf16[1280,1408]{1,0:T(8,128)(2,1)S(1)} %copy-done.48, bf16[1280,1408]{1,0:T(8,128)(2,1)S(1)} %copy-done.47), kind=kOutput, calls=%fused_computation.30 | convolution fusion | flops 7399276544 | bytes 15597568 | tf_op jit(solution)/shard_map/dot_general | solution.py:856
  599.0 23.4 %attend_backward.1 = (bf16[3,1024,512]{2,1,0:T(8,128)(2,1)S(1)}, f32[8,2,512]{2,1,0:T(2,128)S(1)}) custom-call(bf16[3,1024,512]{2,1,0:T(8,128)(2,1)} %copy-done, bf16[1024,512]{1,0:T(8,128)(2,1)S(1)} %maximum_select_fusion.dout_ref, f32[4,2,1024]{2,1,0:T(2,128)S(1)} %get-tuple-element.26.lse_ref, f32[8,2,256,256]{3,2,1,0:T(8,128)} %get-tuple-element.27.tile_ref, ...), custom_call_target="tpu_custom_call" | custom-call | tf_op jit(solution)/shard_map/attend_backward/pallas_call | solution.py:556
  622.4 5.5 fusion.125
  629.2 5.8 convolution_convert_fusion.2
  636.2 18.9 %collective-permute-done.4 = bf16[512,1024]{1,0:T(8,128)(2,1)} collective-permute-done((bf16[512,1024]{1,0:T(8,128)(2,1)}, bf16[512,1024]{1,0:T(8,128)(2,1)}, u32[]{:S(2)}, u32[]{:S(2)}) %collective-permute-start.4) | collective-permute-done | bytes 1048608 | tf_op jit(solution)/shard_map/ppermute | solution.py:717
  655.1 3.0 fusion.26
  658.9 4.6 convolution_convert_fusion.3
  663.5 3.9 copy.102
  667.4 9.5 %add_convert_fusion.1 = bf16[1408,1024]{0,1:T(8,128)(2,1)} fusion(bf16[1408,1024]{0,1:T(8,128)(2,1)} %collective-permute-done.7, bf16[1280,1408]{1,0:T(8,128)(2,1)} %copy-done.13, bf16[1280,1024]{1,0:T(8,128)(2,1)} %bitcast.205), kind=kOutput, calls=%fused_computation.29 | convolution fusion | flops 3695312896 | bytes 11993088 | tf_op jit(solution)/shard_map/dot_general | solution.py:856
  676.9 4.4 all-to-all-start.7
  681.4 6.7 convert_bitcast_fusion
  688.2 7.6 copy.100
  695.8 5.0 copy.111
  700.8 14.4 %add_convert_fusion = bf16[1024,2816]{1,0:T(8,128)(2,1)} fusion(bf16[1024,2816]{1,0:T(8,128)(2,1)} %collective-permute-done.6, bf16[1280,1024]{1,0:T(8,128)(2,1)} %bitcast.18, bf16[1280,1408]{1,0:T(8,128)(2,1)} %get-tuple-element.108, bf16[1280,1408]{1,0:T(8,128)(2,1)} %get-tuple-element.107), kind=kOutput, calls=%fused_computation.2 | convolution fusion | flops 7405043712 | bytes 21364736 | tf_op jit(solution)/shard_map/dot_general | solution.py:856
  716.6 4.7 all-to-all-start.6
  721.4 5.3 copy.92
  726.8 3.9 fusion.29
  730.7 16.8 %psum.7 = f32[1,24,128]{2,1,0:T(8,128)S(1)} all-reduce(f32[1,24,128]{2,1,0:T(8,128)} %reduce-scatter.17.cloned.1.call-done), channel_id=1, replica_groups=mesh['gx'=8,'gy'=4] {'gy'}, use_global_device_ids=true, to_apply=%region_20.21 | all-reduce | flops 3072 | bytes 24576 | tf_op jit(solution)/shard_map/psum | solution.py:954
  749.2 13.9 %reduce-scatter.15.cloned.1.call-done = bf16[128,1024]{1,0:T(8,128)(2,1)} async-done(((bf16[1024,1024]{1,0:T(8,128)(2,1)}), bf16[128,1024]{1,0:T(8,128)(2,1)}) %reduce-scatter.15.cloned.1.call-update) | async-done | bytes 262160
  767.5 43.0 %reduce-scatter.13.cloned.1.call-done = bf16[128,1536]{1,0:T(8,128)(2,1)} async-done(((bf16[1024,1536]{1,0:T(8,128)(2,1)}), bf16[128,1536]{1,0:T(8,128)(2,1)}) %reduce-scatter.13.cloned.1.call-update) | async-done | bytes 393232
  810.5 1.7 reshape.609
  812.6 2.5 collective-permute-start.5
  815.1 17.8 %reduce-scatter.11.cloned.1.call-done = bf16[1,256,128]{2,1,0:T(8,128)(2,1)} async-done(((bf16[4,256,128]{2,1,0:T(8,128)(2,1)}), bf16[1,256,128]{2,1,0:T(8,128)(2,1)}) %reduce-scatter.11.cloned.1.call-update) | async-done | bytes 65552 | tf_op jit(solution)/shard_map/reduce_scatter | solution.py:915
  835.5 13.0 %reshape.597 = f32[4,2,128,2,1408]{4,3,2,1,0:T(2,128)} reshape(bf16[8,128,2816]{2,1,0:T(8,128)(2,1)} %all-to-all-done.6) | data formatting | bytes 17301504 | tf_op jit(solution)/shard_map/convert_element_type | solution.py:867
  848.5 20.3 %copy.125 = f32[4,2,128,2,1408]{4,1,3,2,0:T(2,128)} copy(f32[4,2,128,2,1408]{4,3,2,1,0:T(2,128)} %reshape.597) | data formatting | bytes 23068672 | tf_op jit(solution)/shard_map/convert_element_type | solution.py:867
  868.9 15.3 %reshape.595 = f32[4,128,5632]{2,1,0:T(8,128)} reshape(f32[4,128,2,2,1408]{4,3,2,1,0:T(2,128)} %bitcast.181) | data formatting | bytes 23068672 | tf_op jit(solution)/shard_map/convert_element_type | solution.py:867
  (210 shorter events, 37.9 us)
Async XLA Ops:
  7.2 40.3 %all-to-all-start.2 = ((bf16[8,1408,128]{2,1,0:T(8,128)(2,1)}), bf16[8,1408,128]{2,1,0:T(8,128)(2,1)S(1)}, u32[]{:S(2)}, u32[]{:S(2)}) async-start(bf16[8,1408,128]{2,1,0:T(8,128)(2,1)} %bitcast.198), calls=%async_computation.2 | async-start | bytes 5767168 | tf_op jit(solution)/shard_map/all_to_all | solution.py:782
  47.4 4.9 copy-start.33
  47.4 5.2 copy-start.39
  47.4 5.3 copy-start.32
  47.4 5.3 copy-start.40
  47.4 5.3 copy-start.41
  47.5 156.2 %all-to-all-start.1 = ((bf16[8,128,2816]{1,2,0:T(8,128)(2,1)}), bf16[8,128,2816]{1,2,0:T(8,128)(2,1)}, u32[]{:S(2)}, u32[]{:S(2)}) async-start(bf16[8,128,2816]{1,2,0:T(8,128)(2,1)} %bitcast.182), calls=%async_computation.1 | async-start | bytes 11534336 | tf_op jit(solution)/shard_map/all_to_all | solution.py:784
  154.2 4.5 copy-start.42
  155.2 7.3 copy-start.28
  155.2 43.0 %copy-start.26 = (f32[8,1,128]{2,1,0:T(1,128)}, f32[8,1,128]{2,1,0:T(1,128)S(1)}, u32[]{:S(2)}) copy-start(f32[8,1,128]{2,1,0:T(1,128)S(1)} %get-tuple-element.119) | copy-start | bytes 12292
  162.5 35.6 %copy-start = (bf16[3,1024,512]{2,1,0:T(8,128)(2,1)}, bf16[3,1024,512]{2,1,0:T(8,128)(2,1)S(1)}, u32[]{:S(2)}) copy-start(bf16[3,1024,512]{2,1,0:T(8,128)(2,1)S(1)} %convert_bitcast_fusion.1.proj_ref) | copy-start | bytes 9437188
  162.5 34.3 %copy-start.3 = (bf16[512,1024]{1,0:T(8,128)(2,1)S(1)}, bf16[512,1024]{1,0:T(8,128)(2,1)}, u32[]{:S(2)}) copy-start(bf16[512,1024]{1,0:T(8,128)(2,1)} %tok_ref.1) | copy-start | bytes 3145732
  162.5 34.3 %copy-start.44 = (bf16[1024,1024]{1,0:T(8,128)(2,1)S(1)}, bf16[1024,1024]{1,0:T(8,128)(2,1)}, u32[]{:S(2)}) copy-start(bf16[1024,1024]{1,0:T(8,128)(2,1)} %get-tuple-element.25) | copy-start | bytes 6291460
  182.4 15.7 %copy-start.25 = (bf16[512,512]{1,0:T(8,128)(2,1)}, bf16[512,512]{1,0:T(8,128)(2,1)S(1)}, u32[]{:S(2)}) copy-start(bf16[512,512]{1,0:T(8,128)(2,1)S(1)} %get-tuple-element.113) | copy-start | bytes 1572868
  182.4 14.3 %collective-permute-start = (bf16[512,512]{1,0:T(8,128)(2,1)S(1)}, bf16[512,512]{1,0:T(8,128)(2,1)S(1)}, u32[]{:S(2)}, u32[]{:S(2)}) collective-permute-start(bf16[512,512]{1,0:T(8,128)(2,1)S(1)} %get-tuple-element.114), channel_id=1, source_target_pairs={{0,1},{1,0},{2,3},{3,2},{4,5},{5,4},{6,7},{7,6},{8,9},{9,8},{10,11... | collective-permute-start | bytes 1572872 | tf_op jit(solution)/shard_map/ppermute | solution.py:717
  198.1 5.5 copy-start.30
  203.7 66.3 %all-to-all-start = ((bf16[16,80,1024]{2,1,0:T(8,128)(2,1)}), bf16[16,80,1024]{2,1,0:T(8,128)(2,1)}, u32[]{:S(2)}, u32[]{:S(2)}) async-start(bf16[16,80,1024]{2,1,0:T(8,128)(2,1)} %bitcast.208), calls=%async_computation | async-start | bytes 5242880 | tf_op jit(solution)/shard_map/all_to_all | solution.py:726
  217.2 74.1 %collective-permute-start.1 = (bf16[1024,2816]{1,0:T(8,128)(2,1)}, bf16[1024,2816]{1,0:T(8,128)(2,1)}, u32[]{:S(2)}, u32[]{:S(2)}) collective-permute-start(bf16[1024,2816]{1,0:T(8,128)(2,1)} %bitcast.195), channel_id=1, source_target_pairs={{0,4},{4,0},{8,12},{12,8},{16,20},{20,16},{24,28},{28,24},{1,5},{5... | collective-permute-start | bytes 17301512 | tf_op jit(solution)/shard_map/ppermute | solution.py:721
  219.9 87.7 %collective-permute-start.2 = (bf16[1408,1024]{0,1:T(8,128)(2,1)}, bf16[1408,1024]{0,1:T(8,128)(2,1)S(1)}, u32[]{:S(2)}, u32[]{:S(2)}) collective-permute-start(bf16[1408,1024]{0,1:T(8,128)(2,1)} %bitcast.199), channel_id=1, source_target_pairs={{0,4},{4,0},{8,12},{12,8},{16,20},{20,16},{24,28},{28,24},{1,5},{5... | collective-permute-start | bytes 8650760 | tf_op jit(solution)/shard_map/ppermute | solution.py:721
  281.2 5.8 copy-start.7
  281.2 5.8 copy-start.16
  287.0 4.3 copy-start.13
  302.5 5.1 copy-start.6
  307.6 7.4 copy-start.14
  314.9 6.2 copy-start.9
  314.9 65.5 %all-to-all-start.3 = ((bf16[16,80,1024]{2,1,0:T(8,128)(2,1)}), bf16[16,80,1024]{2,1,0:T(8,128)(2,1)}, u32[]{:S(2)}, u32[]{:S(2)}) async-start(bf16[16,80,1024]{2,1,0:T(8,128)(2,1)} %bitcast.209), calls=%async_computation.3 | async-start | bytes 5242880 | tf_op jit(solution)/shard_map/all_to_all | solution.py:726
  321.1 62.7 %copy-start.37 = (f32[1,16]{1,0:T(1,128)}, f32[1,16]{1,0:T(1,128)S(1)}, u32[]{:S(2)}) copy-start(f32[1,16]{1,0:T(1,128)S(1)} %get-tuple-element.104) | copy-start | bytes 196
  380.4 3.4 copy-start.24
  383.8 5.6 copy-start.20
  391.8 64.4 %copy-start.17 = (bf16[1408,8,128]{0,2,1:T(8,128)(2,1)S(1)}, bf16[1408,8,128]{0,2,1:T(8,128)(2,1)}, u32[]{:S(2)}) copy-start(bf16[1408,8,128]{0,2,1:T(8,128)(2,1)} %copy.85) | copy-start | bytes 8650756
  456.2 14.9 %copy-start.18 = (bf16[16,80,1024]{2,1,0:T(8,128)(2,1)}, bf16[16,80,1024]{2,1,0:T(8,128)(2,1)S(1)}, u32[]{:S(2)}) copy-start(bf16[16,80,1024]{2,1,0:T(8,128)(2,1)S(1)} %all_to_all.40) | copy-start | bytes 7864324
  456.2 28.1 %slice-start = ((s8[14417920]{0:T(1024)(128)(4,1)}), s8[4194304]{0:T(1024)(128)(4,1)S(1)}, s32[]{:S(2)}) async-start(s8[14417920]{0:T(1024)(128)(4,1)} %bitcast.185), calls=%async_computation.16 | async-start | bytes 8388608
  456.2 28.1 %slice-start.1 = ((s8[14417920]{0:T(1024)(128)(4,1)}), s8[4194304]{0:T(1024)(128)(4,1)S(1)}, s32[]{:S(2)}) async-start(s8[14417920]{0:T(1024)(128)(4,1)} %bitcast.185), calls=%async_computation.17 | async-start | bytes 8388608
  456.2 28.1 %slice-start.2 = ((s8[14417920]{0:T(1024)(128)(4,1)}), s8[4194304]{0:T(1024)(128)(4,1)S(1)}, s32[]{:S(2)}) async-start(s8[14417920]{0:T(1024)(128)(4,1)} %bitcast.185), calls=%async_computation.18 | async-start | bytes 8388608
  471.1 13.2 %slice-start.3 = ((s8[14417920]{0:T(1024)(128)(4,1)}), s8[1835008]{0:T(1024)(128)(4,1)S(1)}, s32[]{:S(2)}) async-start(s8[14417920]{0:T(1024)(128)(4,1)} %bitcast.185), calls=%async_computation.19 | async-start | bytes 3670016
  510.7 5.4 copy-start.4
  510.7 65.0 %all-to-all-start.5 = ((bf16[16,80,1024]{2,1,0:T(8,128)(2,1)}), bf16[16,80,1024]{2,1,0:T(8,128)(2,1)}, u32[]{:S(2)}, u32[]{:S(2)}) async-start(bf16[16,80,1024]{2,1,0:T(8,128)(2,1)} %bitcast.207), calls=%async_computation.5 | async-start | bytes 5242880 | tf_op jit(solution)/shard_map/all_to_all | solution.py:726
  515.3 215.4 %reduce-scatter.17.cloned.1.call-start = ((), (), s32[]{:S(2)}) async-start(), calls=%async_computation.15 | async-start | bytes 110592
  575.7 3.5 copy-start.2
  575.7 3.5 copy-start.27
  575.7 3.5 copy-start.31
  579.2 2.2 copy-start.22
  581.4 1.9 copy-start.45
  583.4 2.8 copy-start.47
  583.4 3.9 copy-start.48
  584.8 13.6 %collective-permute-start.3 = (bf16[512,512]{1,0:T(8,128)(2,1)S(1)}, bf16[512,512]{1,0:T(8,128)(2,1)S(1)}, u32[]{:S(2)}, u32[]{:S(2)}) collective-permute-start(bf16[512,512]{1,0:T(8,128)(2,1)S(1)} %get-tuple-element.112), channel_id=1, source_target_pairs={{0,1},{1,0},{2,3},{3,2},{4,5},{5,4},{6,7},{7,6},{8,9},{9,8},{10,11... | collective-permute-start | bytes 1572872 | tf_op jit(solution)/shard_map/ppermute | solution.py:717
  598.4 102.4 %collective-permute-start.6 = (bf16[1024,2816]{1,0:T(8,128)(2,1)}, bf16[1024,2816]{1,0:T(8,128)(2,1)}, u32[]{:S(2)}, u32[]{:S(2)}) collective-permute-start(bf16[1024,2816]{1,0:T(8,128)(2,1)} %convolution_convert_fusion), channel_id=1, source_target_pairs={{0,4},{4,0},{8,12},{12,8},{16,20},{20,16},{24,28},{28,24},{1,5},{5... | collective-permute-start | bytes 17301512 | tf_op jit(solution)/shard_map/ppermute | solution.py:721
  622.3 6.9 copy-start.15
  622.3 6.9 copy-start.19
  627.8 7.2 copy-start.12
  629.2 6.4 copy-start.35
  629.2 25.9 %copy-start.29 = (f32[8,1,128]{2,1,0:T(1,128)S(1)}, f32[8,1,128]{2,1,0:T(1,128)}, u32[]{:S(2)}) copy-start(f32[8,1,128]{2,1,0:T(1,128)} %copy-done.28) | copy-start | bytes 12292
  629.2 25.9 %collective-permute-start.4 = (bf16[512,1024]{1,0:T(8,128)(2,1)}, bf16[512,1024]{1,0:T(8,128)(2,1)}, u32[]{:S(2)}, u32[]{:S(2)}) collective-permute-start(bf16[512,1024]{1,0:T(8,128)(2,1)} %fusion.47), channel_id=1, source_target_pairs={{0,1},{1,0},{2,3},{3,2},{4,5},{5,4},{6,7},{7,6},{8,9},{9,8},{10,11... | collective-permute-start | bytes 3145736 | tf_op jit(solution)/shard_map/ppermute | solution.py:717
  635.1 32.4 %collective-permute-start.7 = (bf16[1408,1024]{0,1:T(8,128)(2,1)}, bf16[1408,1024]{0,1:T(8,128)(2,1)}, u32[]{:S(2)}, u32[]{:S(2)}) collective-permute-start(bf16[1408,1024]{0,1:T(8,128)(2,1)} %convolution_convert_fusion.2), channel_id=1, source_target_pairs={{0,4},{4,0},{8,12},{12,8},{16,20},{20,16},{24,28},{28,24},{1,5},{5... | collective-permute-start | bytes 8650760 | tf_op jit(solution)/shard_map/ppermute | solution.py:721
  658.9 104.3 %reduce-scatter.15.cloned.1.call-start = ((), (), s32[]{:S(2)}) async-start(), calls=%async_computation.14 | async-start | bytes 2359296
  676.9 39.7 %all-to-all-start.7 = ((bf16[8,1408,128]{1,2,0:T(8,128)(2,1)}), bf16[8,1408,128]{1,2,0:T(8,128)(2,1)}, u32[]{:S(2)}, u32[]{:S(2)}) async-start(bf16[8,1408,128]{1,2,0:T(8,128)(2,1)} %bitcast.202), calls=%async_computation.8 | async-start | bytes 5767168 | tf_op jit(solution)/shard_map/all_to_all | solution.py:869
  681.4 129.1 %reduce-scatter.13.cloned.1.call-start = ((), (), s32[]{:S(2)}) async-start(), calls=%async_computation.13 | async-start | bytes 3538944
  716.6 118.9 %all-to-all-start.6 = ((bf16[8,128,2816]{2,1,0:T(8,128)(2,1)}), bf16[8,128,2816]{2,1,0:T(8,128)(2,1)}, u32[]{:S(2)}, u32[]{:S(2)}) async-start(bf16[8,128,2816]{2,1,0:T(8,128)(2,1)} %bitcast.193), calls=%async_computation.7 | async-start | bytes 11534336 | tf_op jit(solution)/shard_map/all_to_all | solution.py:862
  721.3 111.5 %reduce-scatter.11.cloned.1.call-start = ((), (), s32[]{:S(2)}) async-start(), calls=%async_computation.12 | async-start | bytes 327680 | tf_op jit(solution)/shard_map/reduce_scatter | solution.py:915
  721.4 5.3 copy-start.5
  721.4 5.3 copy-start.11
  726.8 21.9 %copy-start.38 = (f32[1,16]{1,0:T(1,128)S(1)}, f32[1,16]{1,0:T(1,128)}, u32[]{:S(2)}) copy-start(f32[1,16]{1,0:T(1,128)} %copy-done.37) | copy-start | bytes 196
  726.8 38.9 %copy-start.36 = (f32[1,16]{1,0:T(1,128)S(1)}, f32[1,16]{1,0:T(1,128)}, u32[]{:S(2)}) copy-start(f32[1,16]{1,0:T(1,128)} %get-tuple-element.103) | copy-start | bytes 196
  812.6 22.0 %collective-permute-start.5 = (bf16[3,128,256]{1,2,0:T(8,128)(2,1)S(1)}, bf16[3,128,256]{1,2,0:T(8,128)(2,1)S(1)}, u32[]{:S(2)}, u32[]{:S(2)}) collective-permute-start(bf16[3,128,256]{1,2,0:T(8,128)(2,1)S(1)} %copy.105), channel_id=1, source_target_pairs={{0,2},{1,3},{2,0},{3,1},{4,6},{5,7},{6,4},{7,5},{8,10},{9,11},{10,... | collective-permute-start | bytes 589832 | tf_op jit(solution)/shard_map/ppermute | solution.py:717
  (8 other events, 10.2 us)
Sparse Core Ops, SparseCore 0:
  659.0 29.7 reduce-scatter.16
  692.0 71.0 reduce-scatter.14
  766.9 43.5 reduce-scatter.12
  813.2 19.5 reduce-scatter.10
where the time goes:
time: 903 us; the launch traced here: 892 us
  waiting for transfers between devices  296 us (33%)
  matrix products  171 us (19%)
  Pallas kernels  139 us (15%)
  local copies, waits for them, and re-layouts  124 us (14%)
  blocking collectives  81.2 us (9%)
  starting transfers between devices  39.6 us (4%)
  other arithmetic  25.4 us (3%)
  between operations  17 us (2%)
    all_to_all x3, waiting for transfers between devices, exchange_slots(): lax.all_to_all(rows, AXES, 0, 0, axis_index_groups=groups, tiled=True)  167 us
    pallas_call x1, Pallas kernels, gather_params(): pl.pallas_call(gather_kernel, out_shape=(jax.ShapeDtypeStruct((2, tok_dev...  95.6 us
    all_to_all x1, blocking collectives, exchange_slots(): lax.all_to_all(rows, AXES, 0, 0, axis_index_groups=groups, tiled=True)  64.4 us
    unnamed x7, waiting for transfers between devices  57 us
    dot_general x7, matrix products, over_rows(): lax.dot_general(left, right, (((0,), (0,)), ((), ())), preferred_element_...  49.2 us
    convert_element_type x3, local copies, waits for them, and re-layouts, fast_device(): grad_inner = grad_inner.reshape(local_experts, 2, shard, 2, quarter).tran...  48.6 us
    unnamed x124, local copies, waits for them, and re-layouts  43.9 us
    ppermute x4, waiting for transfers between devices, swap_z(): return lax.ppermute(values, 'gy', [(i, i ^ step) for i in range(4)])  31.6 us
  transfers between devices with their start and end apart: 19, of which 10 were waited for; matrix products, arithmetic and copies ran while one was open for 20% of the time, Pallas kernels for 16%

commit v1 on v0

--- a/solution.py
+++ b/solution.py
@@ -721,13 +721,316 @@
     return lax.ppermute(values, "gx", [(i, i ^ 1) for i in range(8)])
 
 
-def exchange_slots(rows):
-    groups = [[(2 * c + h) * 4 + z for c in range(4) for z in range(4)] for h in range(2)]
-    return lax.all_to_all(rows, AXES, 0, 0, axis_index_groups=groups, tiled=True)
+def exchange_chips(blocks):
+    groups = [[2 * c + h for c in range(4)] for h in range(2)]
+    return lax.all_to_all(blocks, "gx", 0, 0, axis_index_groups=groups, tiled=True)
 
 
 def geglu(gate_part, up_part):
     return jax.nn.gelu(gate_part, approximate=True) * up_part
+
+
+def expert_kernel(
+    rows_ref, grads_ref, inner_ref, outer_ref,
+    returned_ref, copies_ref, ginner_ref, gouter_ref, inner_in_ref, outer_in_ref, gouter_sum_ref,
+    x_ref, x_t_ref, dy_ref, win_ref, wout_ref, upper_ref, total_ref, back_ref, hid_ref, dup_ref,
+    stage_in_ref, stage_out_ref, add_in_ref, add_out_ref,
+    row_send, row_recv, grad_send, grad_recv, out_send, out_recv, copy_send, copy_recv,
+    w_send, w_recv, part_send, part_recv, gout_send, gout_recv, local_sem,
+):
+    x, z, _, across, sibling = places()
+    core = x % 2
+    chip = x // 2
+    me = chip * 4 + z
+    count, slots, width = x_ref.shape
+    tokens = count * slots
+    tiles = upper_ref.shape[0]
+    half = upper_ref.shape[2] // 2
+    hidden = tiles * half
+    shard = width // 8
+    chunk = tokens // 4
+    f32, bf16 = jnp.float32, jnp.bfloat16
+
+    spots = [lax.rem(me + k, count) for k in range(1, count)]
+    peers = [(2 * (spot // 4) + core, spot % 4) for spot in spots]
+    pair = (sibling, z)
+    barrier = pltpu.get_barrier_semaphore()
+    for peer in peers + [pair]:
+        pl.semaphore_signal(barrier, inc=1, device_id=peer, device_id_type=MESH_ID)
+    pl.semaphore_wait(barrier, len(peers) + 1)
+
+    def remote(source, target, sems, index, device):
+        return pltpu.make_async_remote_copy(
+            src_ref=source, dst_ref=target, send_sem=sems[0].at[index], recv_sem=sems[1].at[index],
+            device_id=device, device_id_type=MESH_ID,
+        )
+
+    def spread(source, target, sems):
+        return [
+            remote(source.at[spot], target.at[me], sems, k, peer)
+            for k, (spot, peer) in enumerate(zip(spots, peers))
+        ]
+
+    def lanes_of(owner):
+        return pl.ds(pl.multiple_of(owner * shard, shard), shard)
+
+    row_copies = spread(rows_ref, x_ref, (row_send, row_recv))
+    for copy in row_copies:
+        copy.start()
+    own_rows = pltpu.make_async_copy(rows_ref.at[me], x_ref.at[me], local_sem.at[0])
+    own_rows.start()
+    own_inner = pltpu.make_async_copy(inner_ref, win_ref.at[:, core], local_sem.at[1])
+    own_inner.start()
+    pair_inner = remote(inner_ref, win_ref.at[:, core], (w_send, w_recv), 0, pair)
+    pair_inner.start()
+    own_outer = pltpu.make_async_copy(outer_ref.at[chip], wout_ref.at[:, lanes_of(x)], local_sem.at[2])
+    own_outer.start()
+    outer_copies = [
+        remote(outer_ref.at[device // 2], wout_ref.at[:, lanes_of(x)], (w_send, w_recv), 1 + j, (device, z))
+        for j, device in enumerate(across)
+    ]
+    for copy in outer_copies:
+        copy.start()
+    own_grads = pltpu.make_async_copy(grads_ref.at[me], dy_ref.at[me], local_sem.at[3])
+    own_grads.start()
+    pair_outer = remote(outer_ref.at[chip], wout_ref.at[:, lanes_of(x)], (w_send, w_recv), 4, pair)
+    pair_outer.start()
+    pair_outer_more = []
+    for j, device in enumerate(across):
+        outer_copies[j].wait_recv()
+        block = wout_ref.at[:, lanes_of(device)]
+        copy = remote(block, block, (w_send, w_recv), 5 + j, pair)
+        copy.start()
+        pair_outer_more.append(copy)
+    for copy in row_copies:
+        copy.wait_send()
+    grad_copies = spread(grads_ref, dy_ref, (grad_send, grad_recv))
+    for copy in grad_copies:
+        copy.start()
+    own_rows.wait()
+    own_inner.wait()
+    own_outer.wait()
+    pair_inner.wait()
+    for copy in outer_copies:
+        copy.wait_send()
+    for copy in [pair_outer] + pair_outer_more:
+        copy.wait()
+    for copy in row_copies:
+        copy.wait_recv()
+
+    def cols(tile, part):
+        return pl.ds(pl.multiple_of(part * hidden + tile * half, half), half)
+
+    def weight(tile, part):
+        return win_ref[:, :, :, cols(tile, part)].reshape(width, half)
+
+    def outer_rows(tile):
+        return wout_ref[pl.ds(pl.multiple_of(tile * half, half), half), :]
+
+    blocks = count // 4
+    total_ref[...] = jnp.zeros_like(total_ref)
+
+    def forward(tile, carry):
+        gate_weight, up_weight, down = weight(tile, 0), weight(tile, 1), outer_rows(tile)
+        for m in range(4):
+            here = pl.ds(m * chunk, chunk)
+            rows = x_ref[m * blocks:(m + 1) * blocks].reshape(chunk, width)
+            gate = dot_nn(rows, gate_weight)
+            up = dot_nn(rows, up_weight)
+            upper_ref[tile, here, :half] = gate.astype(bf16)
+            upper_ref[tile, here, half:] = up.astype(bf16)
+            total_ref[here, :] += dot_nn(geglu(gate, up).astype(bf16), down)
+        return carry
+
+    lax.fori_loop(0, tiles, forward, 0)
+    for m in range(4):
+        back_ref[0, m * blocks:(m + 1) * blocks] = (
+            total_ref[pl.ds(m * chunk, chunk), :].astype(bf16).reshape(blocks, slots, width)
+        )
+    out_copies = spread(back_ref.at[0], returned_ref, (out_send, out_recv))
+    for copy in out_copies:
+        copy.start()
+    own_out = pltpu.make_async_copy(back_ref.at[0, me], returned_ref.at[me], local_sem.at[4])
+    own_out.start()
+    x_t_ref[...] = x_ref[...].reshape(tokens, width).T.reshape(x_t_ref.shape)
+
+    own_grads.wait()
+    for copy in grad_copies:
+        copy.wait()
+    total_ref[...] = jnp.zeros_like(total_ref)
+
+    def backward(tile, carry):
+        gate_weight, up_weight, down = weight(tile, 0), weight(tile, 1), outer_rows(tile)
+        for m in range(4):
+            here = pl.ds(m * chunk, chunk)
+            grads = dy_ref[m * blocks:(m + 1) * blocks].reshape(chunk, width)
+            grad_hidden = dot_nt(grads, down)
+            gate = upper_ref[tile, here, :half].astype(f32)
+            up = upper_ref[tile, here, half:].astype(f32)
+            inner = 0.7978845608028654 * gate * (1.0 + 0.044715 * gate * gate)
+            bent = jnp.tanh(inner)
+            lifted = 0.5 * (1.0 + bent)
+            active = gate * lifted
+            slope = lifted + 0.5 * gate * (1.0 - bent * bent) * (
+                0.7978845608028654 * (1.0 + 3 * 0.044715 * gate * gate)
+            )
+            hid_ref[here, :] = (active * up).astype(bf16)
+            grad_gate = (grad_hidden * up * slope).astype(bf16)
+            grad_up = (grad_hidden * active).astype(bf16)
+            dup_ref[here, :half] = grad_gate
+            dup_ref[here, half:] = grad_up
+            total_ref[here, :] += dot_nt(grad_gate, gate_weight) + dot_nt(grad_up, up_weight)
+        grad_upper = dup_ref[...]
+        other = x_t_ref[:, 1 - core].reshape(width // 2, tokens)
+        part_slot = lax.rem(tile, 2)
+
+        @pl.when(tile >= 2)
+        def _():
+            for copy in parts(tile - 2):
+                copy.wait_send()
+
+        stage_in_ref[part_slot] = dot_nn(other, grad_upper).astype(bf16).reshape(4, shard, 2 * half)
+        grad_down = dot_nn(hid_ref[...].T, dy_ref[...].reshape(tokens, width))
+        for j in range(4):
+            low = grad_down[:, (2 * j) * shard:(2 * j + 1) * shard].astype(bf16)
+            high = grad_down[:, (2 * j + 1) * shard:(2 * j + 2) * shard].astype(bf16)
+            stage_out_ref[part_slot, :, j * shard:(j + 1) * shard] = jnp.where(core == 0, high, low)
+            upper_ref[tile, pl.ds(width // 2, half), j * shard:(j + 1) * shard] = jnp.where(core == 0, low, high)
+        for copy in parts(tile):
+            copy.start()
+        own = x_t_ref[:, core].reshape(width // 2, tokens)
+        upper_ref[tile, pl.ds(0, width // 2), :] = dot_nn(own, grad_upper).astype(bf16)
+        return carry
+
+    def parts(tile):
+        slot = lax.rem(tile, 2)
+        return [
+            remote(stage_in_ref.at[slot], inner_in_ref.at[tile], (part_send, part_recv), 2 * tile, pair),
+            remote(stage_out_ref.at[slot], outer_in_ref.at[tile], (part_send, part_recv), 2 * tile + 1, pair),
+        ]
+
+    lax.fori_loop(0, tiles, backward, 0)
+    for m in range(4):
+        back_ref[1, m * blocks:(m + 1) * blocks] = (
+            total_ref[pl.ds(m * chunk, chunk), :].astype(bf16).reshape(blocks, slots, width)
+        )
+    copy_copies = spread(back_ref.at[1], copies_ref, (copy_send, copy_recv))
+    for copy in copy_copies:
+        copy.start()
+    own_copy = pltpu.make_async_copy(back_ref.at[1, me], copies_ref.at[me], local_sem.at[5])
+    own_copy.start()
+
+    for tile in (tiles - 2, tiles - 1):
+        for copy in parts(tile):
+            copy.wait_send()
+
+    def join(tile, carry):
+        for copy in parts(tile):
+            copy.wait_recv()
+        loads = [
+            pltpu.make_async_copy(inner_in_ref.at[tile], add_in_ref, local_sem.at[6]),
+            pltpu.make_async_copy(outer_in_ref.at[tile], add_out_ref, local_sem.at[7]),
+        ]
+        for copy in loads:
+            copy.start()
+        for copy in loads:
+            copy.wait()
+        own = upper_ref[tile, pl.ds(0, width // 2), :].astype(f32)
+        add_in_ref[...] = (own + add_in_ref[...].reshape(width // 2, 2 * half).astype(f32)).astype(bf16).reshape(
+            add_in_ref.shape
+        )
+        own = upper_ref[tile, pl.ds(width // 2, half), :].astype(f32)
+        add_out_ref[...] = (own + add_out_ref[...].astype(f32)).astype(bf16)
+        stores = [
+            pltpu.make_async_copy(add_in_ref.at[:, :, pl.ds(part * half, half)], ginner_ref.at[:, :, cols(tile, part)], local_sem.at[6 + part])
+            for part in range(2)
+        ] + [
+            pltpu.make_async_copy(
+                add_out_ref, gouter_sum_ref.at[pl.ds(pl.multiple_of(tile * half, half), half), :], local_sem.at[8]
+            )
+        ]
+        for copy in stores:
+            copy.start()
+        for copy in stores:
+            copy.wait()
+        return carry
+
+    lax.fori_loop(0, tiles, join, 0)
+
+    def sums_of(owner):
+        return gouter_sum_ref.at[:, pl.ds(pl.multiple_of((owner // 2) * shard, shard), shard)]
+
+    own_gout = pltpu.make_async_copy(sums_of(x), gouter_ref.at[chip], local_sem.at[9])
+    own_gout.start()
+    gout_copies = [
+        remote(sums_of(device), gouter_ref.at[chip], (gout_send, gout_recv), j, (device, z))
+        for j, device in enumerate(across)
+    ]
+    for copy in gout_copies:
+        copy.start()
+    own_out.wait()
+    own_copy.wait()
+    own_gout.wait()
+    for copy in out_copies + copy_copies + gout_copies:
+        copy.wait()
+
+
+def run_experts(rows, grads, inner, outer):
+    count, slots, width = rows.shape
+    tokens = count * slots
+    hidden = outer.shape[1]
+    half = 256
+    tiles = hidden // half
+    shard = width // 8
+    bf16 = jnp.bfloat16
+    anywhere = pl.BlockSpec(memory_space=pl.ANY)
+    sems = [pltpu.SemaphoreType.DMA((count,))] * 8 + [
+        pltpu.SemaphoreType.DMA((8,)),
+        pltpu.SemaphoreType.DMA((8,)),
+        pltpu.SemaphoreType.DMA((2 * tiles,)),
+        pltpu.SemaphoreType.DMA((2 * tiles,)),
+        pltpu.SemaphoreType.DMA((3,)),
+        pltpu.SemaphoreType.DMA((3,)),
+        pltpu.SemaphoreType.DMA((10,)),
+    ]
+    outs = pl.pallas_call(
+        expert_kernel,
+        out_shape=(
+            jax.ShapeDtypeStruct(rows.shape, bf16),
+            jax.ShapeDtypeStruct(rows.shape, bf16),
+            jax.ShapeDtypeStruct(inner.shape, bf16),
+            jax.ShapeDtypeStruct(outer.shape, bf16),
+            jax.ShapeDtypeStruct((tiles, 4, shard, 2 * half), bf16),
+            jax.ShapeDtypeStruct((tiles, half, 4 * shard), bf16),
+            jax.ShapeDtypeStruct((hidden, 4 * shard), bf16),
+        ),
+        in_specs=[anywhere] * 4,
+        out_specs=(anywhere,) * 7,
+        scratch_shapes=[
+            pltpu.VMEM((count, slots, width), bf16),
+            pltpu.VMEM((4, 2, shard, tokens), bf16),
+            pltpu.VMEM((count, slots, width), bf16),
+            pltpu.VMEM((4, 2, shard, 2 * hidden), bf16),
+            pltpu.VMEM((hidden, width), bf16),
+            pltpu.VMEM((tiles, tokens, 2 * half), bf16),
+            pltpu.VMEM((tokens, width), jnp.float32),
+            pltpu.VMEM((2, count, slots, width), bf16),
+            pltpu.VMEM((tokens, half), bf16),
+            pltpu.VMEM((tokens, 2 * half), bf16),
+            pltpu.VMEM((2, 4, shard, 2 * half), bf16),
+            pltpu.VMEM((2, half, 4 * shard), bf16),
+            pltpu.VMEM((4, shard, 2 * half), bf16),
+            pltpu.VMEM((half, 4 * shard), bf16),
+        ] + sems,
+        compiler_params=pltpu.CompilerParams(
+            collective_id=1, has_side_effects=True, vmem_limit_bytes=63 * 2**20
+        ),
+        cost_estimate=pl.CostEstimate(
+            flops=6 * 3 * tokens * width * hidden, bytes_accessed=60 * 2**20, transcendentals=tokens * hidden
+        ),
+        name="run_experts",
+    )(rows, grads, inner, outer)
+    return outs[:4]
 
 
 def fast_device(
@@ -741,8 +1044,6 @@
     expert_count = router.shape[1]
     top_count = expert_ids.shape[1]
     shard = model_width // 8
-    local_experts, _, upper_width = w_in.shape
-    quarter = upper_width // 4
     bucket_count = rel_bias.shape[0] * 8
     group_heads = rel_bias.shape[1]
 
@@ -775,15 +1076,8 @@
     )
     seq_tokens, qkv_weight, out_weight, smalls = gather_params(tokens, w_qkv, w_out, small)
 
-    inner_sent = (
-        w_in.reshape(local_experts, shard, 2, 2, quarter).transpose(0, 3, 1, 2, 4).reshape(8, shard, 2 * quarter)
-    )
-    outer_sent = w_down.reshape(8, quarter, shard)
-    outer_own = lax.all_to_all(outer_sent, "gx", 0, 0, tiled=True)
-    outer_own = outer_own.transpose(1, 0, 2).reshape(quarter, model_width)
-    inner_own = lax.all_to_all(inner_sent, "gx", 0, 0, tiled=True).reshape(model_width, 2 * quarter)
-    outer_parts = (outer_own, swap_core(outer_own))
-    inner_parts = (inner_own, swap_core(inner_own))
+    inner_own, seq_tokens = lax.optimization_barrier((w_in, seq_tokens))
+    inner_own = exchange_chips(inner_own)
 
     own_small = smalls[0]
     router_t = own_small[:, :16].transpose(1, 0, 2).reshape(expert_count, model_width)
@@ -830,46 +1124,20 @@
         jnp.where(marks[0], gates[0][None], 0.0) + jnp.where(marks[1], gates[1][None], 0.0), axis=1
     )
     send_rows = jnp.dot(dispatch, second_norm, preferred_element_type=f32).astype(bf16)
-    received = exchange_slots(send_rows.reshape(expert_count, CAP, model_width)).reshape(-1, model_width)
     grad_rows = (jnp.dot(dispatch, cotangent, preferred_element_type=f32) * gate_rows[:, None]).astype(bf16)
-    grad_expert = exchange_slots(grad_rows.reshape(expert_count, CAP, model_width)).reshape(-1, model_width)
-
-    uppers = [jnp.dot(received, part, preferred_element_type=f32) for part in inner_parts]
-    hiddens = [geglu(upper[:, :quarter], upper[:, quarter:]).astype(bf16) for upper in uppers]
-    expert_out = sum(
-        jnp.dot(hidden, part, preferred_element_type=f32) for hidden, part in zip(hiddens, outer_parts)
-    ).astype(bf16)
-    returned = exchange_slots(expert_out.reshape(expert_count, CAP, model_width)).reshape(-1, model_width)
-
-    grad_uppers = []
-    for upper, part in zip(uppers, outer_parts):
-        grad_hidden = lax.dot_general(grad_expert, part, (((1,), (1,)), ((), ())), preferred_element_type=f32)
-        _, pull_back = jax.vjp(geglu, upper[:, :quarter], upper[:, quarter:])
-        grad_uppers.append(jnp.concatenate(pull_back(grad_hidden), axis=1).astype(bf16))
-    grad_received = sum(
-        lax.dot_general(grad_upper, part, (((1,), (1,)), ((), ())), preferred_element_type=f32)
-        for grad_upper, part in zip(grad_uppers, inner_parts)
-    ).astype(bf16)
-    grad_copies = exchange_slots(grad_received.reshape(expert_count, CAP, model_width)).reshape(-1, model_width)
+    returned, grad_copies, grad_inner, grad_outer = run_experts(
+        send_rows.reshape(expert_count, CAP, model_width),
+        grad_rows.reshape(expert_count, CAP, model_width),
+        inner_own,
+        w_down,
+    )
+    returned = returned.reshape(-1, model_width)
+    grad_copies = grad_copies.reshape(-1, model_width)
+    grad_inner = exchange_chips(grad_inner).astype(f32)
+    grad_outer = grad_outer.astype(f32)
 
     def over_rows(left, right):
         return lax.dot_general(left, right, (((0,), (0,)), ((), ())), preferred_element_type=f32)
-
-    grad_inner_other = swap_core(over_rows(received, grad_uppers[1]).astype(bf16))
-    grad_outer_other = swap_core(over_rows(hiddens[1], grad_expert).astype(bf16))
-    grad_inner = (over_rows(received, grad_uppers[0]) + grad_inner_other.astype(f32)).astype(bf16)
-    grad_outer = (over_rows(hiddens[0], grad_expert) + grad_outer_other.astype(f32)).astype(bf16)
-    grad_inner = lax.all_to_all(grad_inner.reshape(8, shard, 2 * quarter), "gx", 0, 0, tiled=True)
-    grad_inner = (
-        grad_inner.reshape(local_experts, 2, shard, 2, quarter)
-        .transpose(0, 2, 3, 1, 4)
-        .reshape(local_experts, shard, upper_width)
-        .astype(f32)
-    )
-    grad_outer = lax.all_to_all(
-        grad_outer.reshape(quarter, 8, shard).transpose(1, 0, 2), "gx", 0, 0, tiled=True
-    )
-    grad_outer = grad_outer.reshape(local_experts, 2 * quarter, shard).astype(f32)
 
     picked = [
         lax.dot_general(mark.astype(bf16), returned, (((0,), (0,)), ((), ())), preferred_element_type=f32)

time: 903 us -> 681 us (0.75)
  Pallas kernels: 139 us -> 349 us
  waiting for transfers between devices: 296 us -> 162 us
  matrix products: 171 us -> 39.4 us
  local copies, waits for them, and re-layouts: 124 us -> 38 us
  blocking collectives: 81.2 us -> 17.2 us
  starting transfers between devices: 39.6 us -> 24.7 us
    pallas_call x0 -> x1, Pallas kernels: none -> 258 us  [run_experts(): pl.pallas_call(expert_kernel, out_shape=(jax.ShapeDtypeStruct(rows.shape,...]
    all_to_all x7 -> x2, waiting for transfers between devices: 190 us -> 10.4 us  [exchange_chips(): lax.all_to_all(blocks, 'gx', 0, 0, axis_index_groups=groups, tiled=True)]
    dot_general x8 -> x0, matrix products: 86.9 us -> none  [the longest x2 27.8 us: fast_device(): lax.dot_general(grad_expert, part, (((1,), (1,)), ((), ())), preferred_el...]
    all_to_all x1 -> x0, blocking collectives: 64.4 us -> none  [exchange_slots(): lax.all_to_all(rows, AXES, 0, 0, axis_index_groups=groups, tiled=True)]
    convert_element_type x4 -> x0, local copies, waits for them, and re-layouts: 53.9 us -> none  [the longest x3 48.6 us: fast_device(): grad_inner = grad_inner.reshape(local_experts, 2, shard, 2, quarter).tran...]
    pallas_call x1, Pallas kernels: 95.6 us -> 46.8 us  [gather_params(): pl.pallas_call(gather_kernel, out_shape=(jax.ShapeDtypeStruct((2, tok_dev...]
    unnamed x7, waiting for transfers between devices: 57 us -> 100 us
    dot_general x7 -> x3, matrix products: 49.2 us -> 7.55 us  [over_rows(): lax.dot_general(left, right, (((0,), (0,)), ((), ())), preferred_element_...]
  transfers between devices with their start and end apart: 19 -> 10, of which waited for: 10 -> 8; matrix products, arithmetic and copies ran while one was open for 20% -> 11% of each run, Pallas kernels for 16% -> 3%
where the time goes in v1:
time: 681 us; the launch traced here: 675 us
  Pallas kernels  349 us (51%)
  waiting for transfers between devices  162 us (24%)
  matrix products  39.4 us (6%)
  local copies, waits for them, and re-layouts  38 us (6%)
  other arithmetic  28.2 us (4%)
  starting transfers between devices  24.7 us (4%)
  blocking collectives  17.2 us (3%)
  between operations  16.4 us (2%)
    pallas_call x1, Pallas kernels, run_experts(): pl.pallas_call(expert_kernel, out_shape=(jax.ShapeDtypeStruct(rows.shape,...  258 us
    unnamed x7, waiting for transfers between devices  100 us
    pallas_call x1, Pallas kernels, gather_params(): pl.pallas_call(gather_kernel, out_shape=(jax.ShapeDtypeStruct((2, tok_dev...  46.8 us
    ppermute x4, waiting for transfers between devices, swap_z(): return lax.ppermute(values, 'gy', [(i, i ^ step) for i in range(4)])  33.9 us
    unnamed x69, local copies, waits for them, and re-layouts  25.7 us
    pallas_call x1, Pallas kernels, attend_bwd(): pl.pallas_call(attend_bwd_kernel, grid=(pairs,), out_shape=(jax.ShapeDtyp...  23.7 us
    pallas_call x1, Pallas kernels, attend_fwd(): pl.pallas_call(attend_fwd_kernel, grid=(pairs,), out_shape=(jax.ShapeDtyp...  20 us
    reduce_scatter x1, waiting for transfers between devices, fast_device(): lax.psum_scatter(grad_out_weight, 'gy', scatter_dimension=0, tiled=True)[0]  17.8 us
  transfers between devices with their start and end apart: 10, of which 8 were waited for; matrix products, arithmetic and copies ran while one was open for 11% of the time, Pallas kernels for 3%

profile of v1, /device:TPU:0, one launch (start us, length us, event | category | flops | bytes accessed | tf_op | source)
XLA Modules:
  0.0 674.9 jit_solution(1461061044557764995)
XLA Ops:
  7.2 0.8 fusion.99
  8.2 0.7 pad.21
  8.9 3.1 concatenate.18.small_ref
  12.1 46.8 %gather_params.1 = (bf16[2,512,1024]{2,1,0:T(8,128)(2,1)}, bf16[3,1024,512]{2,1,0:T(8,128)(2,1)}, bf16[1024,1024]{1,0:T(8,128)(2,1)}, bf16[4,8,32,128]{3,2,1,0:T(8,128)(2,1)}) custom-call(bf16[512,1024]{1,0:T(8,128)(2,1)} %tok_ref.1, bf16[3,128,256]{2,1,0:T(8,128)(2,1)} %wq_ref.1, bf16[256,128]{1,0:T(8,128)(2,1)} %wo_ref.1, ...), custom_call_target="tpu_custom_call" | custom-call | tf_op jit(solution)/shard_map/gather_params/pallas_call | solution.py:696
  58.9 5.3 all-to-all-start
  64.3 0.8 fusion.98
  65.0 0.8 slice_bitcast_fusion
  66.6 1.9 fusion.1
  68.9 5.9 convert_bitcast_fusion.1.proj_ref
  74.8 20.0 %attend_forward.1 = (bf16[1024,512]{1,0:T(8,128)(2,1)S(1)}, f32[4,2,1024]{2,1,0:T(2,128)S(1)}, f32[8,2,256,256]{3,2,1,0:T(8,128)}) custom-call(bf16[3,1024,512]{2,1,0:T(8,128)(2,1)S(1)} %convert_bitcast_fusion.1.proj_ref, f32[8,2,512]{2,1,0:T(2,128)S(1)} %reshape.524.span_ref), custom_call_target="tpu_custom_call" | custom-call | tf_op jit(solution)/shard_map/attend_forward/pallas_call | solution.py:458
  94.9 0.6 collective-permute-start
  95.5 0.9 convert_reduce_fusion
  96.5 11.9 %collective-permute-done = bf16[512,512]{1,0:T(8,128)(2,1)S(1)} collective-permute-done((bf16[512,512]{1,0:T(8,128)(2,1)S(1)}, bf16[512,512]{1,0:T(8,128)(2,1)S(1)}, u32[]{:S(2)}, u32[]{:S(2)}) %collective-permute-start) | collective-permute-done | bytes 524320 | tf_op jit(solution)/shard_map/ppermute | solution.py:717
  108.4 1.4 multiply_reduce_fusion.3
  110.4 0.7 copy-done.3
  111.2 0.6 add_reduce_fusion
  111.9 3.1 convolution_convert_fusion
  114.9 3.1 multiply_convert_fusion
  118.1 10.4 %all-to-all-done.inner_ref = bf16[4,128,5632]{2,1,0:T(8,128)(2,1)} async-done(((bf16[4,128,5632]{2,1,0:T(8,128)(2,1)}), bf16[4,128,5632]{2,1,0:T(8,128)(2,1)}, u32[]{:S(2)}, u32[]{:S(2)}) %all-to-all-start) | async-done | bytes 5767200 | tf_op jit(solution)/shard_map/all_to_all | solution.py:726
  128.4 258.3 %run_experts.1 = (bf16[16,80,1024]{2,1,0:T(8,128)(2,1)}, bf16[16,80,1024]{2,1,0:T(8,128)(2,1)}, bf16[4,128,5632]{2,1,0:T(8,128)(2,1)}, bf16[4,2816,128]{2,1,0:T(...) custom-call(bf16[16,80,1024]{2,1,0:T(8,128)(2,1)} %bitcast.181, ...), custom_call_target="tpu_custom_call" | custom-call | flops 66437775360 | bytes 62914560 | tf_op jit(solution)/shard_map/run_experts/pallas_call | solution.py:996
  386.7 3.4 fusion.18
  390.2 1.6 fusion.5
  392.0 3.0 fusion.14
  395.1 0.9 multiply_reduce_fusion.1
  396.6 1.0 copy-done.23
  397.7 1.3 convolution_convert_fusion.2
  399.0 0.9 fusion.96
  399.9 8.7 %collective-permute-start.1 = (bf16[512,512]{1,0:T(8,128)(2,1)}, bf16[512,512]{1,0:T(8,128)(2,1)S(1)}, u32[]{:S(2)}, u32[]{:S(2)}) collective-permute-start(bf16[512,512]{1,0:T(8,128)(2,1)} %get-tuple-element.106), channel_id=1, source_target_pairs={{0,1},{1,0},{2,3},{3,2},{4,5},{5,4},{6,7},{7,6},{8,9},{9,8},{10,11... | collective-permute-start | bytes 1572872 | tf_op jit(solution)/shard_map/ppermute | solution.py:717
  409.1 6.8 %collective-permute-done.1 = bf16[512,512]{1,0:T(8,128)(2,1)S(1)} collective-permute-done((bf16[512,512]{1,0:T(8,128)(2,1)}, bf16[512,512]{1,0:T(8,128)(2,1)S(1)}, u32[]{:S(2)}, u32[]{:S(2)}) %collective-permute-start.1) | collective-permute-done | bytes 524320 | tf_op jit(solution)/shard_map/ppermute | solution.py:717
  415.9 0.8 copy-done.19
  416.7 1.6 maximum_select_fusion.dout_ref
  418.3 23.7 %attend_backward.1 = (bf16[3,1024,512]{2,1,0:T(8,128)(2,1)S(1)}, f32[8,2,512]{2,1,0:T(2,128)S(1)}) custom-call(bf16[3,1024,512]{2,1,0:T(8,128)(2,1)} %copy-done, bf16[1024,512]{1,0:T(8,128)(2,1)S(1)} %maximum_select_fusion.dout_ref, f32[4,2,1024]{2,1,0:T(2,128)S(1)} %get-tuple-element.36.lse_ref, f32[8,2,256,256]{3,2,1,0:T(8,128)} %get-tuple-element.37.tile_ref, ...), custom_call_target="tpu_custom_call" | custom-call | tf_op jit(solution)/shard_map/attend_backward/pallas_call | solution.py:556
  442.0 3.4 fusion.101
  445.5 1.2 fusion.30
  446.7 2.0 collective-permute-start.2
  449.7 15.2 %collective-permute-done.2 = bf16[512,1024]{1,0:T(8,128)(2,1)} collective-permute-done((bf16[512,1024]{1,0:T(8,128)(2,1)}, bf16[512,1024]{1,0:T(8,128)(2,1)}, u32[]{:S(2)}, u32[]{:S(2)}) %collective-permute-start.2) | collective-permute-done | bytes 1048608 | tf_op jit(solution)/shard_map/ppermute | solution.py:717
  464.9 2.7 fusion.9
  467.6 0.7 copy.55
  468.4 3.8 convolution_convert_fusion.1
  472.2 4.1 copy.65
  476.4 6.8 %convert_bitcast_fusion = bf16[3,1024,512]{1,2,0:T(8,128)(2,1)} fusion(bf16[3,1024,512]{2,1,0:T(8,128)(2,1)S(1)} %copy-done.2, bf16[1024,1024]{1,0:T(8,128)(2,1)} %fusion.1), kind=kOutput, calls=%fused_computation.7 | convolution fusion | flops 3222798336 | bytes 8388608 | tf_op jit(solution)/shard_map/td,ctf->cdf/dot_general | solution.py:1186
  483.1 7.6 %copy.63 = bf16[3,1024,512]{2,0,1:T(4,128)(2,1)} copy(bf16[3,1024,512]{1,2,0:T(8,128)(2,1)} %convert_bitcast_fusion) | data formatting | bytes 6291456
  490.8 5.0 copy.74
  495.8 5.4 all-to-all-start.1
  501.4 3.3 convert_element_type.371
  504.7 1.9 copy-done.15
  506.6 3.2 fusion.12
  509.8 10.4 %reduce-scatter.17.cloned.1.call-done = f32[1,24,128]{2,1,0:T(8,128)} async-done(((f32[8,24,128]{2,1,0:T(8,128)}), f32[1,24,128]{2,1,0:T(8,128)}) %reduce-scatter.17.cloned.1.call-update) | async-done | bytes 12304
  520.2 17.2 %psum.7 = f32[1,24,128]{2,1,0:T(8,128)S(1)} all-reduce(f32[1,24,128]{2,1,0:T(8,128)} %reduce-scatter.17.cloned.1.call-done), channel_id=1, replica_groups=mesh['gx'=8,'gy'=4] {'gy'}, use_global_device_ids=true, to_apply=%region_20.21 | all-reduce | flops 3072 | bytes 24576 | tf_op jit(solution)/shard_map/psum | solution.py:1222
  537.4 0.7 dynamic-slice_bitcast_fusion.2
  538.5 0.6 slice_multiply_fusion
  539.2 44.3 %reduce-scatter.15.cloned.1.call-done = bf16[128,1024]{1,0:T(8,128)(2,1)} async-done(((bf16[1024,1024]{1,0:T(8,128)(2,1)}), bf16[128,1024]{1,0:T(8,128)(2,1)}) %reduce-scatter.15.cloned.1.call-update) | async-done | bytes 262160
  583.4 1.1 copy.66
  584.5 0.6 gather_fusion
  585.1 0.8 broadcast_select_fusion
  586.0 0.6 pad_maximum_fusion.3
  587.2 0.6 slice_bitcast_fusion.2
  587.8 45.7 %reduce-scatter.13.cloned.1.call-done = bf16[128,1536]{1,0:T(8,128)(2,1)} async-done(((bf16[1024,1536]{1,0:T(8,128)(2,1)}), bf16[128,1536]{1,0:T(8,128)(2,1)}) %reduce-scatter.13.cloned.1.call-update) | async-done | bytes 393232
  633.4 1.7 reshape.553
  635.5 2.5 collective-permute-start.3
  638.0 17.8 %reduce-scatter.11.cloned.1.call-done = bf16[1,256,128]{2,1,0:T(8,128)(2,1)} async-done(((bf16[4,256,128]{2,1,0:T(8,128)(2,1)}), bf16[1,256,128]{2,1,0:T(8,128)(2,1)}) %reduce-scatter.11.cloned.1.call-update) | async-done | bytes 65552 | tf_op jit(solution)/shard_map/reduce_scatter | solution.py:1183
  655.8 1.5 bitcast_convert_fusion
  657.3 8.6 %convert_element_type.370 = f32[4,128,5632]{2,1,0:T(8,128)} convert(bf16[4,128,5632]{2,1,0:T(8,128)(2,1)} %all-to-all-done.1) | non-fusion elementwise | flops 2883584 | bytes 17301504 | tf_op jit(solution)/shard_map/convert_element_type | solution.py:1136
  666.1 0.9 copy.57
  (118 shorter events, 6.3 us)
Async XLA Ops:
  58.9 7.0 %copy-start.13 = (bf16[2,512,1024]{2,1,0:T(8,128)(2,1)S(1)}, bf16[2,512,1024]{2,1,0:T(8,128)(2,1)}, u32[]{:S(2)}) copy-start(bf16[2,512,1024]{2,1,0:T(8,128)(2,1)} %get-tuple-element.29) | copy-start | bytes 6291460
  58.9 69.6 %all-to-all-start = ((bf16[4,128,5632]{2,1,0:T(8,128)(2,1)}), bf16[4,128,5632]{2,1,0:T(8,128)(2,1)}, u32[]{:S(2)}, u32[]{:S(2)}) async-start(bf16[4,128,5632]{2,1,0:T(8,128)(2,1)} %param.19), calls=%async_computation | async-start | bytes 11534336 | tf_op jit(solution)/shard_map/all_to_all | solution.py:726
  64.2 456.0 %reduce-scatter.17.cloned.1.call-start = ((), (), s32[]{:S(2)}) async-start(), calls=%async_computation.9 | async-start | bytes 110592
  74.8 20.1 %copy-start = (bf16[3,1024,512]{2,1,0:T(8,128)(2,1)}, bf16[3,1024,512]{2,1,0:T(8,128)(2,1)S(1)}, u32[]{:S(2)}) copy-start(bf16[3,1024,512]{2,1,0:T(8,128)(2,1)S(1)} %convert_bitcast_fusion.1.proj_ref) | copy-start | bytes 9437188
  74.8 33.6 %copy-start.5 = (bf16[512,1024]{1,0:T(8,128)(2,1)S(1)}, bf16[512,1024]{1,0:T(8,128)(2,1)}, u32[]{:S(2)}) copy-start(bf16[512,1024]{1,0:T(8,128)(2,1)} %tok_ref.1) | copy-start | bytes 3145732
  74.8 33.6 %copy-start.22 = (bf16[1024,1024]{1,0:T(8,128)(2,1)S(1)}, bf16[1024,1024]{1,0:T(8,128)(2,1)}, u32[]{:S(2)}) copy-start(bf16[1024,1024]{1,0:T(8,128)(2,1)} %get-tuple-element.32) | copy-start | bytes 6291460
  94.9 14.8 %copy-start.20 = (bf16[512,512]{1,0:T(8,128)(2,1)}, bf16[512,512]{1,0:T(8,128)(2,1)S(1)}, u32[]{:S(2)}) copy-start(bf16[512,512]{1,0:T(8,128)(2,1)S(1)} %get-tuple-element.107) | copy-start | bytes 1572868
  94.9 13.4 %collective-permute-start = (bf16[512,512]{1,0:T(8,128)(2,1)S(1)}, bf16[512,512]{1,0:T(8,128)(2,1)S(1)}, u32[]{:S(2)}, u32[]{:S(2)}) collective-permute-start(bf16[512,512]{1,0:T(8,128)(2,1)S(1)} %get-tuple-element.108), channel_id=1, source_target_pairs={{0,1},{1,0},{2,3},{3,2},{4,5},{5,4},{6,7},{7,6},{8,9},{9,8},{10,11... | collective-permute-start | bytes 1572872 | tf_op jit(solution)/shard_map/ppermute | solution.py:717
  108.4 1.4 copy-start.24
  109.7 1.3 copy-start.3
  110.0 4.9 copy-start.8
  111.9 3.1 copy-start.17
  386.7 3.5 copy-start.25
  390.2 1.6 copy-start.4
  390.2 1.8 copy-start.18
  396.1 1.6 copy-start.23
  397.7 1.3 copy-start.10
  399.0 9.8 %copy-start.6 = (bf16[512,1024]{1,0:T(8,128)(2,1)S(1)}, bf16[512,1024]{1,0:T(8,128)(2,1)}, u32[]{:S(2)}) copy-start(bf16[512,1024]{1,0:T(8,128)(2,1)} %tok_ref.1) | copy-start | bytes 3145732
  399.9 16.0 %collective-permute-start.1 = (bf16[512,512]{1,0:T(8,128)(2,1)}, bf16[512,512]{1,0:T(8,128)(2,1)S(1)}, u32[]{:S(2)}, u32[]{:S(2)}) collective-permute-start(bf16[512,512]{1,0:T(8,128)(2,1)} %get-tuple-element.106), channel_id=1, source_target_pairs={{0,1},{1,0},{2,3},{3,2},{4,5},{5,4},{6,7},{7,6},{8,9},{9,8},{10,11... | collective-permute-start | bytes 1572872 | tf_op jit(solution)/shard_map/ppermute | solution.py:717
  415.9 0.8 copy-start.19
  418.3 23.7 %copy-start.21 = (bf16[3,1024,512]{2,1,0:T(8,128)(2,1)S(1)}, bf16[3,1024,512]{2,1,0:T(8,128)(2,1)}, u32[]{:S(2)}) copy-start(bf16[3,1024,512]{2,1,0:T(8,128)(2,1)} %get-tuple-element.27) | copy-start | bytes 9437188
  442.0 3.5 copy-start.1
  445.5 3.6 copy-start.14
  445.5 3.2 copy-start.9
  446.7 18.2 %collective-permute-start.2 = (bf16[512,1024]{1,0:T(8,128)(2,1)}, bf16[512,1024]{1,0:T(8,128)(2,1)}, u32[]{:S(2)}, u32[]{:S(2)}) collective-permute-start(bf16[512,1024]{1,0:T(8,128)(2,1)} %fusion.30), channel_id=1, source_target_pairs={{0,1},{1,0},{2,3},{3,2},{4,5},{5,4},{6,7},{7,6},{8,9},{9,8},{10,11... | collective-permute-start | bytes 3145736 | tf_op jit(solution)/shard_map/ppermute | solution.py:717
  449.7 18.7 %copy-start.11 = (f32[512,1024]{1,0:T(8,128)S(1)}, f32[512,1024]{1,0:T(8,128)}, u32[]{:S(2)}) copy-start(f32[512,1024]{1,0:T(8,128)} %copy-done.10) | copy-start | bytes 6291460
  468.3 115.1 %reduce-scatter.15.cloned.1.call-start = ((), (), s32[]{:S(2)}) async-start(), calls=%async_computation.8 | async-start | bytes 2359296
  472.2 4.2 copy-start.2
  476.3 157.1 %reduce-scatter.13.cloned.1.call-start = ((), (), s32[]{:S(2)}) async-start(), calls=%async_computation.7 | async-start | bytes 3538944
  495.8 5.5 copy-start.16
  495.8 161.5 %all-to-all-start.1 = ((bf16[4,128,5632]{2,1,0:T(8,128)(2,1)}), bf16[4,128,5632]{2,1,0:T(8,128)(2,1)}, u32[]{:S(2)}, u32[]{:S(2)}) async-start(bf16[4,128,5632]{2,1,0:T(8,128)(2,1)} %get-tuple-element.40), calls=%async_computation.2 | async-start | bytes 11534336 | tf_op jit(solution)/shard_map/all_to_all | solution.py:726
  501.2 154.5 %reduce-scatter.11.cloned.1.call-start = ((), (), s32[]{:S(2)}) async-start(), calls=%async_computation.6 | async-start | bytes 327680 | tf_op jit(solution)/shard_map/reduce_scatter | solution.py:1183
  501.3 3.3 copy-start.7
  501.4 3.3 copy-start.12
  501.4 5.2 copy-start.15
  635.5 30.5 %collective-permute-start.3 = (bf16[3,128,256]{1,2,0:T(8,128)(2,1)S(1)}, bf16[3,128,256]{1,2,0:T(8,128)(2,1)S(1)}, u32[]{:S(2)}, u32[]{:S(2)}) collective-permute-start(bf16[3,128,256]{1,2,0:T(8,128)(2,1)S(1)} %copy.68), channel_id=1, source_target_pairs={{0,2},{1,3},{2,0},{3,1},{4,6},{5,7},{6,4},{7,5},{8,10},{9,11},{10,... | collective-permute-start | bytes 589832 | tf_op jit(solution)/shard_map/ppermute | solution.py:717
Sparse Core Ops, SparseCore 0:
  468.4 51.7 reduce-scatter.16
  523.5 59.8 reduce-scatter.14
  587.2 46.2 reduce-scatter.12
  636.1 19.5 reduce-scatter.10
